TPU v7x, 128 devices: a whole 4x4x4 slice. The times are simulated.
128 devices in a mesh: dp: 8 (over x, core), expert: 16 (over z, y).
Axes of the slice: x: 4, y: 4, z: 4, core: 2. Of those that a mesh axis runs over, the one named last changes fastest.
Arguments:
- tokens: bfloat16 [4096, 2048], P(('dp', 'expert')), may hold values from -6 to 6
- self_query: bfloat16 [4096, 2048], P(('dp', 'expert')), may hold values from -160 to 160
- new_kv: bfloat16 [4096, 4096], P(('dp', 'expert')), may hold values from -7 to 7
- kv_cache: bfloat16 [4096, 8, 4096], P(('dp', 'expert')), may hold values from -6 to 6
- parents: int32 [4096], P(('dp', 'expert')), may hold values from 0 to 3, as said below
- dec_len: int32 [1024], P('dp'), may hold values from 1 to 8
- cross_query: bfloat16 [4096, 2048], P(('dp', 'expert')), may hold values from -160 to 160
- memory: bfloat16 [1024, 64, 4096], P(('dp', 'expert')), may hold values from -7 to 7
- src_len: int32 [1024], P(('dp', 'expert')), may hold values from 2 to 64
- norm_gain: float32 [2048], replicated, may hold values from 0.1 to 1.9
- routes: int32 [4096, 2], P(('dp', 'expert')), may hold values from 0 to 15, all different within a row; in each aligned block of 32 rows (0 to 31, 32 to 63, ...) at most 8 rows name the same one
- gate_weights: float32 [4096, 2], P(('dp', 'expert')), may hold values from 0.2 to 1
- expert_in: bfloat16 [16, 2048, 8192], P('expert', None, 'dp'), may hold values from -0.125 to 0.125
- expert_out: bfloat16 [16, 8192, 2048], P('expert', 'dp'), may hold values from -0.0625 to 0.0625
Outputs:
- mixed: bfloat16 [4096, 2048], P(('dp', 'expert'))
- new_cache: bfloat16 [4096, 8, 4096], P(('dp', 'expert'))
Inputs may be any that keep to these rules, and one draw needn't show every extreme that they name: `parents`: within the rows of one device at most 16 name the same parent beam, and one beam is named by exactly 16 of them. `routes`: A row names two different experts; within the rows of one device no expert is named more than 8 times.
All inputs are finite; a program needn't handle non-finite values.
Results may differ from a plain program's by a relative error of at most 0.014.
Values may be sent and summed in bfloat16 or wider, within the bound.
A program may use at most 128 MiB of HBM per device.

v0:
```python
import math

import jax
import jax.numpy as jnp
from jax import lax
from jax.sharding import PartitionSpec as P

HEAD = 128
BEAM = 4


def shifted(value, axis, steps):
    count = lax.axis_size(axis)
    pairs = [(source, (source + steps) % count) for source in range(count)]
    return lax.ppermute(value, axis, pairs)


def per_device(
    tokens,
    self_query,
    new_kv,
    kv_cache,
    parents,
    dec_len,
    cross_query,
    memory,
    src_len,
    norm_gain,
    routes,
    gate_weights,
    expert_in,
    expert_out,
):
    row_count, model_width = tokens.shape
    head_count = model_width // HEAD
    scale = 1.0 / math.sqrt(HEAD)
    expert_count = lax.axis_size("expert")
    group = expert_count // BEAM
    expert_pos = lax.axis_index("expert")
    my_beam = expert_pos // group
    sub_pos = expert_pos % group
    span = kv_cache.shape[1]
    flat_cache = kv_cache.reshape(row_count, -1)
    new_flat = jnp.where((parents == my_beam)[:, None], flat_cache, jnp.zeros((), flat_cache.dtype))
    for offset in range(1, BEAM):
        arrived = shifted(flat_cache, "expert", offset * group)
        from_beam = (my_beam - offset) % BEAM
        new_flat = jnp.where((parents == from_beam)[:, None], arrived, new_flat)
    new_cache = new_flat.reshape(kv_cache.shape)
    queries = self_query.reshape(row_count, head_count, HEAD)
    keys = new_cache[:, :, :model_width].reshape(row_count, span, head_count, HEAD)
    values = new_cache[:, :, model_width:].reshape(row_count, span, head_count, HEAD)
    own_key = new_kv[:, :model_width].reshape(row_count, head_count, HEAD)
    own_value = new_kv[:, model_width:].reshape(row_count, head_count, HEAD)
    scores = jnp.einsum("rhk,rphk->rhp", queries, keys, preferred_element_type=jnp.float32) * scale
    own = jnp.einsum("rhk,rhk->rh", queries, own_key, preferred_element_type=jnp.float32) * scale
    lengths = lax.dynamic_slice_in_dim(dec_len, sub_pos * row_count, row_count)
    valid = (jnp.arange(span, dtype=jnp.int32)[None, :] < lengths[:, None])[:, None, :]
    peak = jnp.maximum(jnp.max(jnp.where(valid, scores, -1e30), -1), own)
    cache_terms = jnp.where(valid, jnp.exp(scores - peak[..., None]), 0.0)
    own_term = jnp.exp(own - peak)
    total = jnp.sum(cache_terms, -1) + own_term
    cache_weights = (cache_terms / total[..., None]).astype(jnp.bfloat16)
    own_weight = (own_term / total).astype(jnp.bfloat16)
    self_out = jnp.einsum(
        "rhp,rphk->rhk", cache_weights, values, preferred_element_type=jnp.float32
    )
    self_out = (
        self_out + own_weight.astype(jnp.float32)[..., None] * own_value.astype(jnp.float32)
    ).reshape(row_count, model_width)
    quarter = row_count // BEAM
    owner_sub = expert_pos // BEAM
    owner_part = expert_pos % BEAM
    gathered = lax.all_gather(cross_query, "expert", axis=0, tiled=True).reshape(
        BEAM, group, BEAM, quarter, model_width
    )
    picked_q = lax.dynamic_index_in_dim(gathered, owner_sub, 1, keepdims=False)
    picked_q = lax.dynamic_index_in_dim(picked_q, owner_part, 1, keepdims=False)
    local_len = memory.shape[1]
    cross_q = picked_q.reshape(BEAM, quarter, head_count, HEAD)
    mem_keys = memory[:, :, :model_width].reshape(quarter, local_len, head_count, HEAD)
    mem_values = memory[:, :, model_width:].reshape(quarter, local_len, head_count, HEAD)
    cross_scores = (
        jnp.einsum("bshk,sphk->bshp", cross_q, mem_keys, preferred_element_type=jnp.float32) * scale
    )
    reach = (jnp.arange(local_len, dtype=jnp.int32)[None, :] < src_len[:, None])[None, :, None, :]
    cross_peak = jnp.max(jnp.where(reach, cross_scores, -1e30), -1)
    cross_terms = jnp.where(reach, jnp.exp(cross_scores - cross_peak[..., None]), 0.0)
    cross_weights = cross_terms / jnp.sum(cross_terms, -1)[..., None]
    owner_out = jnp.einsum(
        "bshp,sphk->bshk",
        cross_weights,
        mem_values.astype(jnp.float32),
        precision=lax.Precision.HIGHEST,
    )
    owner_out = owner_out.reshape(BEAM, quarter, model_width)
    back_box = jnp.zeros((BEAM, group, quarter, model_width), jnp.float32)
    back_box = lax.dynamic_update_index_in_dim(back_box, owner_out, owner_sub, 1)
    came_back = lax.all_to_all(
        back_box.reshape(expert_count, quarter, model_width).astype(jnp.bfloat16),
        "expert",
        split_axis=0,
        concat_axis=0,
        tiled=True,
    ).astype(jnp.float32)
    cross_out = lax.dynamic_index_in_dim(
        came_back.reshape(group, BEAM, quarter, model_width), sub_pos, 0, keepdims=False
    )
    cross_out = cross_out.reshape(row_count, model_width)
    hidden = tokens.astype(jnp.float32) + self_out + cross_out
    row_mean = jnp.mean(hidden, -1, keepdims=True)
    centered = hidden - row_mean
    variance = jnp.mean(centered * centered, -1, keepdims=True)
    moe_in = (centered * lax.rsqrt(variance + 1e-05) * norm_gain).astype(jnp.bfloat16)
    slot_cap = 4 * row_count // expert_count
    flat_routes = routes.reshape(-1)
    onehot = (flat_routes[:, None] == jnp.arange(expert_count, dtype=jnp.int32)[None, :]).astype(
        jnp.int32
    )
    before = jnp.cumsum(onehot, 0) - onehot
    rank_in = jnp.sum(before * onehot, 1)
    target_slot = flat_routes * slot_cap + rank_in
    slot_table = (
        jnp.arange(expert_count * slot_cap, dtype=jnp.int32)[:, None] == target_slot[None, :]
    ).astype(jnp.bfloat16)
    doubled = jnp.repeat(moe_in, 2, axis=0)
    outgoing_rows = jnp.dot(slot_table, doubled, preferred_element_type=jnp.float32).astype(
        jnp.bfloat16
    )
    outgoing_rows = outgoing_rows.reshape(expert_count, slot_cap, model_width)
    block = lax.all_to_all(outgoing_rows, "expert", split_axis=0, concat_axis=0, tiled=True)
    items = block.shape[1]
    stacked = block.reshape(expert_count * items, model_width)
    inner = jax.nn.relu(
        jnp.dot(
            lax.all_gather(stacked, "dp", axis=0, tiled=True),
            expert_in[0],
            preferred_element_type=jnp.float32,
        )
    ).astype(jnp.bfloat16)
    summed = lax.psum_scatter(
        jnp.dot(inner, expert_out[0], preferred_element_type=jnp.float32).astype(jnp.bfloat16),
        "dp",
        scatter_dimension=0,
        tiled=True,
    )
    returned = lax.all_to_all(
        summed.reshape(expert_count, items, model_width),
        "expert",
        split_axis=0,
        concat_axis=0,
        tiled=True,
    )
    per_slot = jnp.dot(
        slot_table.T,
        returned.reshape(expert_count * slot_cap, model_width),
        preferred_element_type=jnp.float32,
    )
    per_slot = per_slot.reshape(row_count, 2, model_width)
    mixed = hidden + jnp.sum(gate_weights[..., None] * per_slot, 1)
    return (mixed.astype(jnp.bfloat16), new_cache)


def solution(mesh):
    placed = (
        P(("dp", "expert"), None),
        P(("dp", "expert"), None),
        P(("dp", "expert"), None),
        P(("dp", "expert"), None, None),
        P(("dp", "expert")),
        P("dp"),
        P(("dp", "expert"), None),
        P(("dp", "expert"), None, None),
        P(("dp", "expert")),
        P(),
        P(("dp", "expert"), None),
        P(("dp", "expert"), None),
        P("expert", None, "dp"),
        P("expert", "dp", None),
    )
    return jax.shard_map(
        per_device,
        mesh=mesh,
        in_specs=placed,
        out_specs=(P(("dp", "expert"), None), P(("dp", "expert"), None, None)),
        check_vma=False,
    )
```

profile of v0, /device:TPU:0, one launch (start us, length us, event | category | flops | bytes accessed | tf_op | source)
XLA Modules:
  0.0 275.9 jit_solution(14484925481398382891)
XLA Ops:
  7.2 0.0 all-gather.3.cloned.1.call-start
  7.2 2.8 %copy.53 = bf16[4,8,8,4096]{3,1,2,0:T(8,128)(2,1)S(1)} copy(bf16[4,8,8,4096]{3,2,1,0:T(8,128)(2,1)} %bitcast.115) | data formatting | bytes 4194304
  10.0 0.0 copy-start.9
  10.0 0.0 copy-start.12
  10.1 0.0 copy-start.13
  10.1 0.0 copy-start.10
  10.1 4.2 %collective-permute-start = (bf16[32,32768]{1,0:T(8,128)(2,1)S(1)}, bf16[32,32768]{1,0:T(8,128)(2,1)}, u32[]{:S(2)}, u32[]{:S(2)}) collective-permute-start(bf16[32,32768]{1,0:T(8,128)(2,1)S(1)} %bitcast.110), channel_id=1, source_target_pairs={{0,12},{1,13},{2,14},{3,15},{4,0},{5,1},{6,2},{7,3},{8,4},{9,5},{1... | collective-permute-start | bytes 6291464 | tf_op jit(solution)/shard_map/ppermute | solution.py:15
  14.3 1.3 collective-permute-start.2
  15.5 0.0 all-gather.3.cloned.1.call-update
  15.6 0.2 reshape.199
  16.0 0.1 fusion.37
  16.1 0.1 copy.46
  16.2 0.1 copy.57
  16.3 0.1 copy.39
  16.3 0.1 reshape.182
  16.5 0.1 fusion.44
  16.5 0.1 reduce_window_sum.11
  16.7 0.1 dynamic_slice.13
  16.7 0.2 select_reduce_fusion.2
  16.9 0.1 iota_compare_fusion.4
  17.0 4.8 %slice_bitcast_fusion.1 = (bf16[8,8,16,8,128]{4,3,2,1,0:T(8,128)(2,1)}, bf16[8,8,16,8,128]{4,3,2,1,0:T(8,128)(2,1)}) fusion(bf16[8,64,4096]{2,1,0:T(8,128)(2,1)} %param.21), kind=kLoop, calls=%fused_computation.17 | loop fusion | bytes 8388608
  21.9 84.3 %collective-permute-done = bf16[32,32768]{1,0:T(8,128)(2,1)} collective-permute-done((bf16[32,32768]{1,0:T(8,128)(2,1)S(1)}, bf16[32,32768]{1,0:T(8,128)(2,1)}, u32[]{:S(2)}, u32[]{:S(2)}) %collective-permute-start) | collective-permute-done | bytes 2097184 | tf_op jit(solution)/shard_map/ppermute | solution.py:15
  106.2 3.4 %collective-permute-done.2 = bf16[32,32768]{1,0:T(8,128)(2,1)} collective-permute-done((bf16[32,32768]{1,0:T(8,128)(2,1)S(1)}, bf16[32,32768]{1,0:T(8,128)(2,1)}, u32[]{:S(2)}, u32[]{:S(2)}) %collective-permute-start.2) | collective-permute-done | bytes 2097184 | tf_op jit(solution)/shard_map/ppermute | solution.py:15
  109.6 3.3 %select_select_fusion = bf16[32,32768]{1,0:T(8,128)(2,1)S(1)} fusion(bf16[32,32768]{1,0:T(8,128)(2,1)} %collective-permute-done, bf16[32,32768]{1,0:T(8,128)(2,1)} %collective-permute-done.1, bf16[32,32768]{1,0:T(8,128)(2,1)} %collective-permute-done.2, bf16[32,32768]{1,0:T(8,128)(2,1)S(1)} %bitcast.113, pred[32]{0:T(512)(128)(4,1)S(1)} %get-tuple-element.12, ...), kind=kLoop, calls=%fused_computation.18 | loop fusion | flops 4194304 | bytes 10485888 | tf_op jit(solution)/shard_map/jit(_where)/select_n | solution.py:48
  112.9 1.2 copy.54
  114.1 0.0 copy-start.1
  114.1 1.3 copy-done.1
  115.4 0.7 fusion.30
  116.1 0.2 copy.42
  116.4 0.4 copy.47
  116.8 0.1 copy.32
  116.9 16.4 %all-gather.3.cloned.1.call-done = bf16[512,2048]{1,0:T(8,128)(2,1)} async-done(((bf16[32,2048]{1,0:T(8,128)(2,1)}), bf16[512,2048]{1,0:T(8,128)(2,1)}) %all-gather.3.cloned.1.call-update) | async-done | bytes 2097168 | tf_op jit(solution)/shard_map/all_gather | solution.py:74
  133.3 1.1 dynamic-slice_bitcast_fusion
  134.4 1.2 fusion.21
  135.5 0.4 fusion.52
  135.9 1.8 fusion.24
  137.8 0.1 broadcast_in_dim.110
  137.8 0.8 broadcast_in_dim.106
  138.7 0.7 bitcast_dynamic-update-slice_fusion
  139.3 4.9 %all-to-all-start = ((bf16[16,8,2048]{2,1,0:T(8,128)(2,1)}), bf16[16,8,2048]{2,1,0:T(8,128)(2,1)S(1)}, u32[]{:S(2)}, u32[]{:S(2)}) async-start(bf16[16,8,2048]{2,1,0:T(8,128)(2,1)} %bitcast.10), calls=%async_computation | async-start | bytes 1048576 | tf_op jit(solution)/shard_map/all_to_all | solution.py:99
  144.3 0.0 copy-start.7
  144.3 0.0 all-gather.5.cloned.1.call-start
  144.4 0.7 fusion.31
  145.1 0.1 fusion.36
  145.2 9.6 %all-to-all-done = bf16[16,8,2048]{2,1,0:T(8,128)(2,1)S(1)} async-done(((bf16[16,8,2048]{2,1,0:T(8,128)(2,1)}), bf16[16,8,2048]{2,1,0:T(8,128)(2,1)S(1)}, u32[]{:S(2)}, u32[]{:S(2)}) %all-to-all-start) | async-done | bytes 524320 | tf_op jit(solution)/shard_map/all_to_all | solution.py:99
  154.8 0.2 fusion.50
  155.0 0.2 multiply_reduce_fusion
  155.2 0.1 multiply_convert_fusion
  155.4 0.1 broadcast_in_dim.111
  155.5 0.1 reshape.183
  155.6 0.3 fusion.8
  155.9 13.4 %all_to_all.15 = bf16[16,8,2048]{2,1,0:T(8,128)(2,1)} all-to-all(bf16[16,8,2048]{2,1,0:T(8,128)(2,1)S(1)} %fusion.8), channel_id=1, replica_groups=mesh['dp'=8,'expert'=16] {'expert'}, dimensions={0} | all-to-all | bytes 1048576 | tf_op jit(solution)/shard_map/all_to_all | solution.py:131
  169.3 0.0 all-gather.5.cloned.1.call-update
  169.3 0.2 reduce-scatter.2.cloned.1.call-start
  169.6 29.5 %all-gather.5.cloned.1.call-done = bf16[1024,2048]{1,0:T(8,128)(2,1)} async-done(((bf16[128,2048]{1,0:T(8,128)(2,1)}), bf16[1024,2048]{1,0:T(8,128)(2,1)}) %all-gather.5.cloned.1.call-update) | async-done | bytes 4194320 | tf_op jit(solution)/shard_map/all_gather | solution.py:136
  199.1 8.1 %maximum_convert_fusion = bf16[1024,1024]{1,0:T(8,128)(2,1)S(1)} fusion(bf16[1024,2048]{1,0:T(8,128)(2,1)} %all-gather.5.cloned.1.call-done, bf16[1,2048,1024]{2,1,0:T(8,128)(2,1)} %param.26), kind=kOutput, calls=%fused_computation.5 | convolution fusion | flops 4297064448 | bytes 10485760 | tf_op jit(solution)/shard_map/dot_general | solution.py:135
  207.2 6.1 %fusion.5 = bf16[1024,2048]{1,0:T(8,128)(2,1)} fusion(bf16[1024,1024]{1,0:T(8,128)(2,1)S(1)} %maximum_convert_fusion, bf16[1,1024,2048]{2,1,0:T(8,128)(2,1)S(1)} %copy-done.11), kind=kOutput, calls=%fused_computation.6 | convolution fusion | flops 4297064448 | bytes 10485760 | tf_op jit(solution)/shard_map/dot_general | solution.py:142
  213.3 0.0 reduce-scatter.2.cloned.1.call-update
  213.3 38.0 %reduce-scatter.2.cloned.1.call-done = bf16[128,2048]{1,0:T(8,128)(2,1)} async-done(((bf16[1024,2048]{1,0:T(8,128)(2,1)}), bf16[128,2048]{1,0:T(8,128)(2,1)}) %reduce-scatter.2.cloned.1.call-update) | async-done | bytes 524304 | tf_op jit(solution)/shard_map/reduce_scatter | solution.py:141
  251.4 7.0 %all-to-all-start.2 = ((bf16[16,8,2048]{2,1,0:T(8,128)(2,1)}), bf16[16,8,2048]{2,1,0:T(8,128)(2,1)S(1)}, u32[]{:S(2)}, u32[]{:S(2)}) async-start(bf16[16,8,2048]{2,1,0:T(8,128)(2,1)} %bitcast.123), calls=%async_computation.3 | async-start | bytes 1048576 | tf_op jit(solution)/shard_map/all_to_all | solution.py:147
  258.3 0.1 iota_compare_fusion.3
  258.4 10.0 %all-to-all-done.2 = bf16[16,8,2048]{2,1,0:T(8,128)(2,1)S(1)} async-done(((bf16[16,8,2048]{2,1,0:T(8,128)(2,1)}), bf16[16,8,2048]{2,1,0:T(8,128)(2,1)S(1)}, u32[]{:S(2)}, u32[]{:S(2)}) %all-to-all-start.2) | async-done | bytes 524320 | tf_op jit(solution)/shard_map/all_to_all | solution.py:147
  268.5 0.2 fusion.17
  268.7 0.7 add_convert_fusion
  (39 shorter events, 0.3 us)
Async XLA Ops:
  7.2 126.1 %all-gather.3.cloned.1.call-start = ((), (), s32[]{:S(2)}) async-start(), calls=%async_computation.4 | async-start | bytes 2228224 | tf_op jit(solution)/shard_map/all_gather | solution.py:74
  7.2 8.4 %copy-start.4 = (bf16[32,2048]{1,0:T(8,128)(2,1)S(1)}, bf16[32,2048]{1,0:T(8,128)(2,1)}, u32[]{:S(2)}) copy-start(bf16[32,2048]{1,0:T(8,128)(2,1)} %param.15) | copy-start | bytes 393220
  7.2 8.6 %copy-start.5 = (bf16[32,4096]{1,0:T(8,128)(2,1)S(1)}, bf16[32,4096]{1,0:T(8,128)(2,1)}, u32[]{:S(2)}) copy-start(bf16[32,4096]{1,0:T(8,128)(2,1)} %param.16) | copy-start | bytes 786436
  10.0 6.2 %copy-start.9 = (s32[32,2]{0,1:T(2,128)S(1)}, s32[32,2]{0,1:T(2,128)}, u32[]{:S(2)}) copy-start(s32[32,2]{0,1:T(2,128)} %param.24) | copy-start | bytes 772
  10.0 6.6 %copy-start.12 = (s32[128]{0:T(128)S(1)}, s32[128]{0:T(128)}, u32[]{:S(2)}) copy-start(s32[128]{0:T(128)} %param.19) | copy-start | bytes 1540
  10.1 6.9 %copy-start.13 = (s32[8]{0:T(128)S(1)}, s32[8]{0:T(128)}, u32[]{:S(2)}) copy-start(s32[8]{0:T(128)} %param.22) | copy-start | bytes 100
  10.1 7.0 %copy-start.10 = (s32[32]{0:T(128)S(1)}, s32[32]{0:T(128)}, u32[]{:S(2)}) copy-start(s32[32]{0:T(128)} %param.18) | copy-start | bytes 388
  10.1 96.1 %collective-permute-start = (bf16[32,32768]{1,0:T(8,128)(2,1)S(1)}, bf16[32,32768]{1,0:T(8,128)(2,1)}, u32[]{:S(2)}, u32[]{:S(2)}) collective-permute-start(bf16[32,32768]{1,0:T(8,128)(2,1)S(1)} %bitcast.110), channel_id=1, source_target_pairs={{0,12},{1,13},{2,14},{3,15},{4,0},{5,1},{6,2},{7,3},{8,4},{9,5},{1... | collective-permute-start | bytes 6291464 | tf_op jit(solution)/shard_map/ppermute | solution.py:15
  14.3 91.9 %collective-permute-start.1 = (bf16[32,32768]{1,0:T(8,128)(2,1)S(1)}, bf16[32,32768]{1,0:T(8,128)(2,1)}, u32[]{:S(2)}, u32[]{:S(2)}) collective-permute-start(bf16[32,32768]{1,0:T(8,128)(2,1)S(1)} %bitcast.111), channel_id=1, source_target_pairs={{0,8},{1,9},{2,10},{3,11},{4,12},{5,13},{6,14},{7,15},{8,0},{9,1},... | collective-permute-start | bytes 6291464 | tf_op jit(solution)/shard_map/ppermute | solution.py:15
  14.3 95.4 %collective-permute-start.2 = (bf16[32,32768]{1,0:T(8,128)(2,1)S(1)}, bf16[32,32768]{1,0:T(8,128)(2,1)}, u32[]{:S(2)}, u32[]{:S(2)}) collective-permute-start(bf16[32,32768]{1,0:T(8,128)(2,1)S(1)} %bitcast.112), channel_id=1, source_target_pairs={{0,4},{1,5},{2,6},{3,7},{4,8},{5,9},{6,10},{7,11},{8,12},{9,13},{1... | collective-permute-start | bytes 6291464 | tf_op jit(solution)/shard_map/ppermute | solution.py:15
  114.1 1.3 copy-start.1
  114.1 20.3 %copy-start = (bf16[8,8,16,8,128]{4,3,2,1,0:T(8,128)(2,1)S(1)}, bf16[8,8,16,8,128]{4,3,2,1,0:T(8,128)(2,1)}, u32[]{:S(2)}) copy-start(bf16[8,8,16,8,128]{4,3,2,1,0:T(8,128)(2,1)} %get-tuple-element.4) | copy-start | bytes 6291460
  133.3 2.7 copy-start.3
  137.7 6.6 %copy-start.2 = (bf16[4,8,8,4096]{3,2,1,0:T(8,128)(2,1)S(1)}, bf16[4,8,8,4096]{3,2,1,0:T(8,128)(2,1)}, u32[]{:S(2)}) copy-start(bf16[4,8,8,4096]{3,2,1,0:T(8,128)(2,1)} %copy-done.1) | copy-start | bytes 6291460
  138.7 16.1 %copy-start.6 = (bf16[32,2048]{1,0:T(8,128)(2,1)S(1)}, bf16[32,2048]{1,0:T(8,128)(2,1)}, u32[]{:S(2)}) copy-start(bf16[32,2048]{1,0:T(8,128)(2,1)} %param.14) | copy-start | bytes 393220
  139.3 15.5 %all-to-all-start = ((bf16[16,8,2048]{2,1,0:T(8,128)(2,1)}), bf16[16,8,2048]{2,1,0:T(8,128)(2,1)S(1)}, u32[]{:S(2)}, u32[]{:S(2)}) async-start(bf16[16,8,2048]{2,1,0:T(8,128)(2,1)} %bitcast.10), calls=%async_computation | async-start | bytes 1048576 | tf_op jit(solution)/shard_map/all_to_all | solution.py:99
  144.3 10.9 %copy-start.7 = (f32[2048]{0:T(1024)S(1)}, f32[2048]{0:T(1024)}, u32[]{:S(2)}) copy-start(f32[2048]{0:T(1024)} %param.23) | copy-start | bytes 24580
  144.3 54.8 %all-gather.5.cloned.1.call-start = ((), (), s32[]{:S(2)}) async-start(), calls=%async_computation.5 | async-start | bytes 4718592 | tf_op jit(solution)/shard_map/all_gather | solution.py:136
  169.3 82.0 %reduce-scatter.2.cloned.1.call-start = ((), (), s32[]{:S(2)}) async-start(), calls=%async_computation.6 | async-start | bytes 4718592 | tf_op jit(solution)/shard_map/reduce_scatter | solution.py:141
  199.1 8.1 %copy-start.11 = (bf16[1,1024,2048]{2,1,0:T(8,128)(2,1)S(1)}, bf16[1,1024,2048]{2,1,0:T(8,128)(2,1)}, u32[]{:S(2)}) copy-start(bf16[1,1024,2048]{2,1,0:T(8,128)(2,1)} %param.27) | copy-start | bytes 12582916
  213.3 55.2 %copy-start.8 = (f32[32,2]{0,1:T(2,128)S(1)}, f32[32,2]{0,1:T(2,128)}, u32[]{:S(2)}) copy-start(f32[32,2]{0,1:T(2,128)} %param.25) | copy-start | bytes 772
  251.4 17.1 %all-to-all-start.2 = ((bf16[16,8,2048]{2,1,0:T(8,128)(2,1)}), bf16[16,8,2048]{2,1,0:T(8,128)(2,1)S(1)}, u32[]{:S(2)}, u32[]{:S(2)}) async-start(bf16[16,8,2048]{2,1,0:T(8,128)(2,1)} %bitcast.123), calls=%async_computation.3 | async-start | bytes 1048576 | tf_op jit(solution)/shard_map/all_to_all | solution.py:147
Sparse Core Ops, SparseCore 0:
  15.7 117.5 all-gather.2
  169.5 29.5 all-gather.4
  213.4 37.8 reduce-scatter.1
where the time goes:
time: 276 us
  waiting for transfers between devices  191 us (69%)
  matrix products  19 us (7%)
  starting transfers between devices  17.7 us (6%)
  local copies, waits for them, and re-layouts  14.3 us (5%)
  between operations  14.3 us (5%)
  blocking collectives  13.4 us (5%)
  other arithmetic  5.81 us (2%)
    ppermute x3, waiting for transfers between devices, shifted(): return lax.ppermute(value, axis, pairs)  87.8 us
    reduce_scatter x1, waiting for transfers between devices, per_device(): lax.psum_scatter(jnp.dot(inner, expert_out[0], preferred_element_type=jnp...  38 us
    all_gather x1, waiting for transfers between devices, per_device(): lax.all_gather(stacked, 'dp', axis=0, tiled=True)  29.5 us
    all_gather x1, waiting for transfers between devices, per_device(): lax.all_gather(cross_query, 'expert', axis=0, tiled=True)  16.4 us
    all_to_all x1, blocking collectives, per_device(): lax.all_to_all(outgoing_rows, 'expert', split_axis=0, concat_axis=0, tile...  13.4 us
    unnamed x37, local copies, waits for them, and re-layouts  11.4 us
    all_to_all x1, waiting for transfers between devices, per_device(): lax.all_to_all(summed.reshape(expert_count, items, model_width), 'expert'...  10 us
    all_to_all x1, waiting for transfers between devices, per_device(): lax.all_to_all(back_box.reshape(expert_count, quarter, model_width).astyp...  9.62 us
  transfers between devices with their start and end apart: 8, of which 7 were waited for; matrix products, arithmetic and copies ran while one was open for 5% of the time, Pallas kernels for 0%

commit v1 on v0

v1 whole, which is shorter than its diff:
```python
import functools
import math

import jax
import jax.numpy as jnp
from jax import lax
from jax.experimental import pallas as pl
from jax.experimental.pallas import tpu as pltpu
from jax.sharding import PartitionSpec as P

HEAD = 128
BEAM = 4
GROUP = 4
CHIPS = 4
EXPERTS = 16
PAGE_CAP = 16
MESH = pl.DeviceIdType.MESH
ANY = pl.BlockSpec(memory_space=pl.ANY)
DMA = pltpu.SemaphoreType.DMA


def place():
    dp = lax.axis_index("dp")
    ex = lax.axis_index("expert")
    return dp, ex, lax.div(ex, GROUP), lax.rem(ex, GROUP)


def send(src, dst, send_sem, recv_sem, dp, ex):
    return pltpu.make_async_remote_copy(
        src_ref=src,
        dst_ref=dst,
        send_sem=send_sem,
        recv_sem=recv_sem,
        device_id=(dp, ex),
        device_id_type=MESH,
    )


def greet(barrier, dp, ex):
    pl.semaphore_signal(barrier, inc=1, device_id=(dp, ex), device_id_type=MESH)


def ask_kernel(
    query, cross, parents, queries, crosses, wishes,
    local, q_send, q_recv, p_send, p_recv, c_send, c_recv,
):
    dp, ex, z, y = place()
    barrier = pltpu.get_barrier_semaphore()
    for off in range(1, BEAM):
        greet(barrier, dp, lax.rem(z + off, BEAM) * GROUP + y)
    for beam in range(BEAM):
        pl.when(beam * GROUP + z != ex)(functools.partial(greet, barrier, dp, beam * GROUP + z))
    pl.semaphore_wait(barrier, jnp.where(z == y, 6, 7))

    crossing = [
        send(cross.at[p], crosses.at[z], c_send.at[p], c_recv.at[z], dp, y * GROUP + p)
        for p in range(GROUP)
    ]
    for p in range(GROUP):
        pl.when(y * GROUP + p != ex)(crossing[p].start)
    moves = []
    for off in (1, 3, 2):
        peer = lax.rem(z + off, BEAM) * GROUP + y
        moves.append(send(parents, wishes.at[z], p_send.at[off - 1], p_recv.at[off - 1], dp, peer))
        moves.append(send(query, queries.at[z], q_send.at[off - 1], q_recv.at[off - 1], dp, peer))
    for move in moves:
        move.start()
    stays = [
        pltpu.make_async_copy(query, queries.at[z], local.at[0]),
        pltpu.make_async_copy(parents, wishes.at[z], local.at[1]),
    ]
    for stay in stays:
        stay.start()
    own = pltpu.make_async_copy(cross.at[y], crosses.at[z], local.at[2])
    pl.when(z == y)(own.start)
    pl.when(z == y)(own.wait)
    for stay in stays:
        stay.wait()
    for move in moves:
        move.wait()
    for p in range(GROUP):
        pl.when(y * GROUP + p != ex)(crossing[p].wait_send)
    for beam in range(BEAM):
        coming = send(cross.at[0], crosses.at[beam], c_send.at[0], c_recv.at[beam], dp, beam * GROUP + z)
        pl.when(beam * GROUP + z != ex)(coming.wait_recv)


def ask(query, cross, parents):
    shapes = [jax.ShapeDtypeStruct((BEAM,) + a.shape, a.dtype) for a in (query, cross[0], parents)]
    return pl.pallas_call(
        ask_kernel,
        out_shape=shapes,
        in_specs=[ANY] * 3,
        out_specs=[ANY] * 3,
        scratch_shapes=[DMA((3,))] + [DMA((3,))] * 4 + [DMA((4,))] * 2,
        compiler_params=pltpu.CompilerParams(collective_id=0, has_side_effects=True),
        name="ask",
    )(query, cross, parents)


def answer_kernel(
    outs, stats, cross, got, got_stats, crosses,
    local, o_send, o_recv, t_send, t_recv, c_send, c_recv,
):
    dp, ex, z, y = place()
    barrier = pltpu.get_barrier_semaphore()
    for off in range(1, BEAM):
        greet(barrier, dp, lax.rem(z + off, BEAM) * GROUP + y)
    for p in range(GROUP):
        pl.when(y * GROUP + p != ex)(functools.partial(greet, barrier, dp, y * GROUP + p))
    pl.semaphore_wait(barrier, jnp.where(z == y, 6, 7))

    crossing = [
        send(cross.at[beam], crosses.at[y], c_send.at[beam], c_recv.at[y], dp, beam * GROUP + z)
        for beam in range(BEAM)
    ]
    for beam in range(BEAM):
        pl.when(beam * GROUP + z != ex)(crossing[beam].start)
    moves = []
    for off in (1, 3, 2):
        other = lax.rem(z + off, BEAM)
        peer = other * GROUP + y
        moves.append(send(stats.at[other], got_stats.at[z], t_send.at[off - 1], t_recv.at[off - 1], dp, peer))
        moves.append(send(outs.at[other], got.at[z], o_send.at[off - 1], o_recv.at[off - 1], dp, peer))
    for move in moves:
        move.start()
    stays = [
        pltpu.make_async_copy(outs.at[z], got.at[z], local.at[0]),
        pltpu.make_async_copy(stats.at[z], got_stats.at[z], local.at[1]),
    ]
    for stay in stays:
        stay.start()
    own = pltpu.make_async_copy(cross.at[z], crosses.at[y], local.at[2])
    pl.when(z == y)(own.start)
    pl.when(z == y)(own.wait)
    for stay in stays:
        stay.wait()
    for move in moves:
        move.wait()
    for beam in range(BEAM):
        pl.when(beam * GROUP + z != ex)(crossing[beam].wait_send)
    for p in range(GROUP):
        coming = send(cross.at[0], crosses.at[p], c_send.at[0], c_recv.at[p], dp, y * GROUP + p)
        pl.when(y * GROUP + p != ex)(coming.wait_recv)


def answer(outs, stats, cross):
    shapes = [jax.ShapeDtypeStruct(a.shape, a.dtype) for a in (outs, stats, cross)]
    return pl.pallas_call(
        answer_kernel,
        out_shape=shapes,
        in_specs=[ANY] * 3,
        out_specs=[ANY] * 3,
        scratch_shapes=[DMA((3,))] + [DMA((3,))] * 4 + [DMA((4,))] * 2,
        compiler_params=pltpu.CompilerParams(collective_id=1, has_side_effects=True),
        name="answer",
    )(outs, stats, cross)


def pack_kernel(wishes, cache, packed, sems):
    _, _, z, _ = place()
    rows = cache.shape[0]

    def each(act):
        for off in range(1, BEAM):
            asker = lax.rem(z + off, BEAM)

            def one(row, count):
                wanted = wishes[asker, row] == z
                page = pltpu.make_async_copy(
                    cache.at[row], packed.at[off - 1, count], sems.at[off - 1, row]
                )
                pl.when(wanted)(lambda: act(page))
                return count + wanted.astype(jnp.int32)

            lax.fori_loop(0, rows, one, jnp.int32(0))

    each(lambda page: page.start())
    each(lambda page: page.wait())


def pack(wishes, cache):
    return pl.pallas_call(
        pack_kernel,
        out_shape=jax.ShapeDtypeStruct((BEAM - 1, PAGE_CAP) + cache.shape[1:], cache.dtype),
        in_specs=[pl.BlockSpec(memory_space=pltpu.SMEM), ANY],
        out_specs=ANY,
        scratch_shapes=[DMA((BEAM - 1, cache.shape[0]))],
        name="pack",
    )(wishes, cache)


def unpack_kernel(parents, cache, arrived, fresh, sem):
    _, _, z, _ = place()
    rows = cache.shape[0]

    def begin(row, counts):
        parent = parents[row]
        off = lax.rem(z - parent + BEAM, BEAM)

        def keep():
            pltpu.make_async_copy(cache.at[row], fresh.at[row], sem).start()

        pl.when(off == 0)(keep)
        after = []
        for step in range(1, BEAM):
            hit = off == step

            def take(step=step):
                pltpu.make_async_copy(arrived.at[step - 1, counts[step - 1]], fresh.at[row], sem).start()

            pl.when(hit)(take)
            after.append(counts[step - 1] + hit.astype(jnp.int32))
        return tuple(after)

    lax.fori_loop(0, rows, begin, (jnp.int32(0),) * (BEAM - 1))
    pltpu.make_async_copy(cache, fresh, sem).wait()


def unpack(parents, cache, arrived):
    return pl.pallas_call(
        unpack_kernel,
        out_shape=jax.ShapeDtypeStruct(cache.shape, cache.dtype),
        in_specs=[pl.BlockSpec(memory_space=pltpu.SMEM), ANY, ANY],
        out_specs=ANY,
        scratch_shapes=[DMA],
        name="unpack",
    )(parents, cache, arrived)


ORDER = (0, 1, 3, 2)
OWN, LEFT, RIGHT, OPPOSITE = range(4)


def expert_kernel(
    slots, first, second, pages, returned, arrived,
    held, first_v, second_v, picked, inner, total, to_twin, from_twin, to_chip, from_chip, result,
    w_sem, local, d_send, d_recv, r_send, r_recv,
    g_send, g_recv, o_send, o_recv, t_send, t_recv,
    y_send, y_recv, x_send, x_recv, p_send, p_recv,
):
    dp, ex, z, y = place()
    x, core = lax.div(dp, 2), lax.rem(dp, 2)
    twin = x * 2 + 1 - core
    chip = [x, lax.rem(x + CHIPS - 1, CHIPS), lax.rem(x + 1, CHIPS), lax.rem(x + 2, CHIPS)]
    width = slots.shape[-1]
    hidden = first.shape[-1]
    block = EXPERTS * slots.shape[1]

    barrier = pltpu.get_barrier_semaphore()
    for a in range(BEAM):
        for b in range(GROUP):
            if a or b:
                greet(barrier, dp, lax.rem(z + a, BEAM) * GROUP + lax.rem(y + b, GROUP))
    greet(barrier, twin, ex)
    for side in (LEFT, RIGHT, OPPOSITE):
        greet(barrier, chip[side] * 2 + core, ex)
    loads = [
        pltpu.make_async_copy(first, first_v, w_sem.at[0]),
        pltpu.make_async_copy(second, second_v, w_sem.at[1]),
    ]
    for load in loads:
        load.start()
    pl.semaphore_wait(barrier, EXPERTS - 1 + 4)

    def peer(a, b):
        return lax.rem(z + a, BEAM) * GROUP + lax.rem(y + b, GROUP)

    def source(a, b):
        return lax.rem(z + BEAM - a, BEAM) * GROUP + lax.rem(y + GROUP - b, GROUP)

    home = held.at[x, core]
    stay = pltpu.make_async_copy(slots.at[ex], home.at[ex], local.at[0])
    stay.start()
    sent = []
    for a in ORDER:
        for b in range(GROUP):
            if a or b:
                spot = a * GROUP + b
                move = send(slots.at[peer(a, b)], home.at[ex], d_send.at[spot], d_recv.at[spot], dp, peer(a, b))
                move.start()
                sent.append(move)

    def chunk(which, owner, j):
        zz = lax.rem(z + BEAM - ORDER[j], BEAM)
        return held.at[chip[which], owner, pl.ds(zz * GROUP, GROUP)]

    def to_sibling(which, j):
        part = chunk(which, core, j)
        move = send(part, part, t_send.at[which, j], t_recv.at[which, j], twin, ex)
        move.start()
        sent.append(move)

    def from_sibling(which):
        for j in range(4):
            part = chunk(which, 1 - core, j)
            send(part, part, t_send.at[which, j], t_recv.at[which, j], twin, ex).wait_recv()

    stay.wait()
    for j, a in enumerate(ORDER):
        for b in range(GROUP):
            if a or b:
                spot = a * GROUP + b
                there = home.at[source(a, b)]
                send(there, there, d_send.at[spot], d_recv.at[spot], dp, source(a, b)).wait_recv()
        part = chunk(OWN, core, j)
        for way, side in ((0, RIGHT), (1, LEFT)):
            move = send(part, part, g_send.at[way, j], g_recv.at[way, j], chip[side] * 2 + core, ex)
            move.start()
            sent.append(move)
        to_sibling(OWN, j)

    paged = []
    for off in (1, 3, 2):
        move = send(
            pages.at[off - 1], arrived.at[off - 1], p_send.at[off - 1], p_recv.at[off - 1],
            dp, lax.rem(z + off, BEAM) * GROUP + y,
        )
        move.start()
        paged.append(move)

    def project(which):
        cells = picked.shape[0] // 2
        for half, owner in ((0, core), (1, 1 - core)):
            picked[half * cells : (half + 1) * cells, :] = held[chip[which], owner].reshape(cells, width)
        tile = min(256, hidden)

        @pl.loop(0, hidden // tile)
        def _(n):
            spot = pl.ds(pl.multiple_of(n * tile, tile), tile)
            part = jnp.dot(picked[...], first_v[:, spot], preferred_element_type=jnp.float32)
            inner[:, spot] = jnp.maximum(part, 0.0).astype(inner.dtype)

        wide = min(256, width)

        @pl.loop(0, width // wide)
        def _(n):
            spot = pl.ds(pl.multiple_of(n * wide, wide), wide)
            part = jnp.dot(inner[...], second_v[:, spot], preferred_element_type=jnp.float32)
            total[which, :, spot] = part[:cells]
            to_twin[which, :, spot] = part[cells:].astype(to_twin.dtype)

        move = send(to_twin.at[which], from_twin.at[which], y_send.at[which], y_recv.at[which], twin, ex)
        move.start()
        sent.append(move)

    def forward(which):
        there = from_twin.at[which]
        send(there, there, y_send.at[which], y_recv.at[which], twin, ex).wait_recv()
        wide = min(256, width)

        @pl.loop(0, width // wide)
        def _(n):
            spot = pl.ds(pl.multiple_of(n * wide, wide), wide)
            both = total[which, :, spot] + from_twin[which, :, spot].astype(jnp.float32)
            to_chip[which - 1, :, spot] = both.astype(to_chip.dtype)

        move = send(
            to_chip.at[which - 1], from_chip.at[which - 1], x_send.at[which - 1], x_recv.at[which - 1],
            chip[which] * 2 + core, ex,
        )
        move.start()
        sent.append(move)

    def landed(way, j):
        side = LEFT if way == 0 else RIGHT
        part = chunk(side, core, j)
        send(part, part, g_send.at[way, j], g_recv.at[way, j], dp, ex).wait_recv()
        to_sibling(side, j)
        if (j < 2) == (way == 0):
            onward = RIGHT if way == 0 else LEFT
            move = send(part, part, o_send.at[j], o_recv.at[j], chip[onward] * 2 + core, ex)
            move.start()
            sent.append(move)

    for load in loads:
        load.wait()
    from_sibling(OWN)
    project(OWN)
    for j in range(4):
        landed(0, j)
        landed(1, j)
    from_sibling(LEFT)
    project(LEFT)
    from_sibling(RIGHT)
    project(RIGHT)
    forward(LEFT)
    forward(RIGHT)
    for j in range(4):
        part = chunk(OPPOSITE, core, j)
        send(part, part, o_send.at[j], o_recv.at[j], dp, ex).wait_recv()
        to_sibling(OPPOSITE, j)
    from_sibling(OPPOSITE)
    project(OPPOSITE)
    forward(OPPOSITE)

    there = from_twin.at[OWN]
    send(there, there, y_send.at[OWN], y_recv.at[OWN], twin, ex).wait_recv()
    for which in (LEFT, RIGHT, OPPOSITE):
        there = from_chip.at[which - 1]
        send(there, there, x_send.at[which - 1], x_recv.at[which - 1], dp, ex).wait_recv()
    wide = min(256, width)

    @pl.loop(0, width // wide)
    def _(n):
        spot = pl.ds(pl.multiple_of(n * wide, wide), wide)
        whole = total[OWN, :, spot] + from_twin[OWN, :, spot].astype(jnp.float32)
        for which in (LEFT, RIGHT, OPPOSITE):
            whole = whole + from_chip[which - 1, :, spot].astype(jnp.float32)
        result[:, :, spot] = whole.astype(result.dtype).reshape(EXPERTS, block // EXPERTS, wide)

    stay = pltpu.make_async_copy(result.at[ex], returned.at[ex], local.at[1])
    stay.start()
    for a in (2, 1, 3, 0):
        for b in range(GROUP):
            if a or b:
                spot = a * GROUP + b
                move = send(result.at[peer(a, b)], returned.at[ex], r_send.at[spot], r_recv.at[spot], dp, peer(a, b))
                move.start()
                sent.append(move)
    stay.wait()
    for a in range(BEAM):
        for b in range(GROUP):
            if a or b:
                spot = a * GROUP + b
                there = returned.at[source(a, b)]
                send(there, there, r_send.at[spot], r_recv.at[spot], dp, source(a, b)).wait_recv()
    for move in sent:
        move.wait_send()
    for move in paged:
        move.wait()


def experts(slots, first, second, pages):
    count, cap, width = slots.shape
    hidden = first.shape[-1]
    block = count * cap
    kind = slots.dtype
    scratch = [
        pltpu.VMEM((CHIPS, 2, count, cap, width), kind),
        pltpu.VMEM(first.shape, kind),
        pltpu.VMEM(second.shape, kind),
        pltpu.VMEM((2 * block, width), kind),
        pltpu.VMEM((2 * block, hidden), kind),
        pltpu.VMEM((4, block, width), jnp.float32),
        pltpu.VMEM((4, block, width), kind),
        pltpu.VMEM((4, block, width), kind),
        pltpu.VMEM((3, block, width), kind),
        pltpu.VMEM((3, block, width), kind),
        pltpu.VMEM((count, cap, width), kind),
    ]
    sems = [
        DMA((2,)), DMA((2,)), DMA((16,)), DMA((16,)), DMA((16,)), DMA((16,)),
        DMA((2, 4)), DMA((2, 4)), DMA((4,)), DMA((4,)), DMA((4, 4)), DMA((4, 4)),
        DMA((4,)), DMA((4,)), DMA((3,)), DMA((3,)), DMA((3,)), DMA((3,)),
    ]
    return pl.pallas_call(
        expert_kernel,
        out_shape=[
            jax.ShapeDtypeStruct(slots.shape, kind),
            jax.ShapeDtypeStruct(pages.shape, pages.dtype),
        ],
        in_specs=[ANY] * 4,
        out_specs=[ANY] * 2,
        scratch_shapes=scratch + sems,
        compiler_params=pltpu.CompilerParams(
            collective_id=2, has_side_effects=True, vmem_limit_bytes=48 * 2**20
        ),
        name="experts",
    )(slots, first, second, pages)


def per_device(
    tokens,
    self_query,
    new_kv,
    kv_cache,
    parents,
    dec_len,
    cross_query,
    memory,
    src_len,
    norm_gain,
    routes,
    gate_weights,
    expert_in,
    expert_out,
):
    row_count, model_width = tokens.shape
    head_count = model_width // HEAD
    scale = 1.0 / math.sqrt(HEAD)
    expert_pos = lax.axis_index("expert")
    sub_pos = expert_pos % GROUP
    span = kv_cache.shape[1]
    quarter = row_count // BEAM

    queries, cross_q, wishes = ask(
        self_query, cross_query.reshape(GROUP, quarter, model_width), parents.reshape(1, row_count)
    )
    pages = pack(wishes.reshape(BEAM, row_count), kv_cache)

    keys = kv_cache[:, :, :model_width].reshape(row_count, span, head_count, HEAD)
    values = kv_cache[:, :, model_width:].reshape(row_count, span, head_count, HEAD)
    asked = queries.reshape(BEAM, row_count, head_count, HEAD)
    lengths = lax.dynamic_slice_in_dim(dec_len, sub_pos * row_count, row_count)
    valid = (jnp.arange(span, dtype=jnp.int32)[None, :] < lengths[:, None])[None, :, None, :]
    scores = jnp.einsum("brhk,rphk->brhp", asked, keys, preferred_element_type=jnp.float32) * scale
    peak = jnp.max(jnp.where(valid, scores, -1e30), -1)
    terms = jnp.where(valid, jnp.exp(scores - peak[..., None]), 0.0)
    mass = jnp.sum(terms, -1)
    weights = (terms / mass[..., None]).astype(jnp.bfloat16)
    outs = jnp.einsum("brhp,rphk->brhk", weights, values, preferred_element_type=jnp.float32)
    outs = outs.astype(jnp.bfloat16).reshape(BEAM, row_count, model_width)
    stats = jnp.pad(peak + jnp.log(mass), ((0, 0), (0, 0), (0, HEAD - head_count)))

    local_len = memory.shape[1]
    cross_q = cross_q.reshape(BEAM, quarter, head_count, HEAD)
    mem_keys = memory[:, :, :model_width].reshape(quarter, local_len, head_count, HEAD)
    mem_values = memory[:, :, model_width:].reshape(quarter, local_len, head_count, HEAD)
    cross_scores = (
        jnp.einsum("bshk,sphk->bshp", cross_q, mem_keys, preferred_element_type=jnp.float32) * scale
    )
    reach = (jnp.arange(local_len, dtype=jnp.int32)[None, :] < src_len[:, None])[None, :, None, :]
    cross_peak = jnp.max(jnp.where(reach, cross_scores, -1e30), -1)
    cross_terms = jnp.where(reach, jnp.exp(cross_scores - cross_peak[..., None]), 0.0)
    cross_weights = cross_terms / jnp.sum(cross_terms, -1)[..., None]
    owner_out = jnp.einsum(
        "bshp,sphk->bshk",
        cross_weights.astype(jnp.bfloat16),
        mem_values,
        preferred_element_type=jnp.float32,
    )
    owner_out = owner_out.astype(jnp.bfloat16).reshape(BEAM, quarter, model_width)

    got, got_stats, cross_out = answer(outs, stats, owner_out)

    own_key = new_kv[:, :model_width].reshape(row_count, head_count, HEAD)
    own_value = new_kv[:, model_width:].reshape(row_count, head_count, HEAD)
    own = (
        jnp.einsum(
            "rhk,rhk->rh",
            self_query.reshape(row_count, head_count, HEAD),
            own_key,
            preferred_element_type=jnp.float32,
        )
        * scale
    )
    chosen = parents[None, :] == jnp.arange(BEAM, dtype=jnp.int32)[:, None]
    cached = jnp.sum(jnp.where(chosen[..., None], got.astype(jnp.float32), 0.0), 0)
    level = jnp.sum(jnp.where(chosen[..., None], got_stats[..., :head_count], 0.0), 0)
    top = jnp.maximum(level, own)
    part = jnp.exp(level - top)
    own_part = jnp.exp(own - top)
    cache_share = part / (part + own_part)
    own_share = own_part / (part + own_part)
    self_out = (
        cache_share[..., None] * cached.reshape(row_count, head_count, HEAD)
        + own_share[..., None] * own_value.astype(jnp.float32)
    ).reshape(row_count, model_width)
    cross_out = cross_out.reshape(row_count, model_width).astype(jnp.float32)

    hidden = tokens.astype(jnp.float32) + self_out + cross_out
    row_mean = jnp.mean(hidden, -1, keepdims=True)
    centered = hidden - row_mean
    variance = jnp.mean(centered * centered, -1, keepdims=True)
    moe_in = (centered * lax.rsqrt(variance + 1e-05) * norm_gain).astype(jnp.bfloat16)

    slot_cap = 4 * row_count // EXPERTS
    named = routes[:, :, None] == jnp.arange(EXPERTS, dtype=jnp.int32)[None, None, :]
    per_row = jnp.sum(named.astype(jnp.int32), 1)
    before = jnp.cumsum(per_row, 0) - per_row
    slot = jnp.sum(jnp.where(named, before[:, None, :], 0), -1) + routes * slot_cap
    places = jnp.arange(EXPERTS * slot_cap, dtype=jnp.int32)
    taken = (slot[:, :, None] == places[None, None, :]).astype(jnp.bfloat16)
    table = (taken[:, 0] + taken[:, 1]).T
    slots = jnp.dot(table, moe_in, preferred_element_type=jnp.float32).astype(jnp.bfloat16)

    returned, arrived = experts(
        slots.reshape(EXPERTS, slot_cap, model_width), expert_in[0], expert_out[0], pages
    )
    per_slot = jnp.einsum(
        "rks,sd->rkd",
        taken,
        returned.reshape(EXPERTS * slot_cap, model_width),
        preferred_element_type=jnp.float32,
    )
    mixed = hidden + jnp.sum(gate_weights[..., None] * per_slot, 1)
    return (mixed.astype(jnp.bfloat16), unpack(parents, kv_cache, arrived))


def solution(mesh):
    placed = (
        P(("dp", "expert"), None),
        P(("dp", "expert"), None),
        P(("dp", "expert"), None),
        P(("dp", "expert"), None, None),
        P(("dp", "expert")),
        P("dp"),
        P(("dp", "expert"), None),
        P(("dp", "expert"), None, None),
        P(("dp", "expert")),
        P(),
        P(("dp", "expert"), None),
        P(("dp", "expert"), None),
        P("expert", None, "dp"),
        P("expert", "dp", None),
    )
    return jax.shard_map(
        per_device,
        mesh=mesh,
        in_specs=placed,
        out_specs=(P(("dp", "expert"), None), P(("dp", "expert"), None, None)),
        check_vma=False,
    )
```

time: 276 us -> 283 us (1.025)
  Pallas kernels: 0 us -> 257 us
  waiting for transfers between devices: 191 us -> 0 us
  starting transfers between devices: 17.7 us -> 0 us
  blocking collectives: 13.4 us -> 0 us
  between operations: 14.3 us -> 1.02 us
  matrix products: 19 us -> 7.86 us
  local copies, waits for them, and re-layouts: 14.3 us -> 10.8 us
    pallas_call x0 -> x5, Pallas kernels: none -> 257 us  [the longest x1 108 us: experts(): pl.pallas_call(expert_kernel, out_shape=[jax.ShapeDtypeStruct(slots.shape...]
    ppermute x3 -> x0, waiting for transfers between devices: 87.8 us -> none  [shifted(): return lax.ppermute(value, axis, pairs)]
    all_gather x2 -> x0, waiting for transfers between devices: 45.9 us -> none  [the longest x1 29.5 us: per_device(): lax.all_gather(stacked, 'dp', axis=0, tiled=True)]
    reduce_scatter x1 -> x0, waiting for transfers between devices: 38 us -> none  [per_device(): lax.psum_scatter(jnp.dot(inner, expert_out[0], preferred_element_type=jnp...]
    all_to_all x2 -> x0, waiting for transfers between devices: 19.7 us -> none  [the longest x1 10 us: per_device(): lax.all_to_all(summed.reshape(expert_count, items, model_width), 'expert'...]
    all_to_all x1 -> x0, blocking collectives: 13.4 us -> none  [per_device(): lax.all_to_all(outgoing_rows, 'expert', split_axis=0, concat_axis=0, tile...]
    all_to_all x2 -> x0, starting transfers between devices: 11.9 us -> none  [the longest x1 6.97 us: per_device(): lax.all_to_all(summed.reshape(expert_count, items, model_width), 'expert'...]
    dot_general x7 -> x5, matrix products: 17.9 us -> 6.68 us  [the longest x1 3.11 us: per_device(): jnp.einsum('brhp,rphk->brhk', weights, values, preferred_element_type=jnp...]
  transfers between devices with their start and end apart: 8 -> 0, of which waited for: 7 -> 0; matrix products, arithmetic and copies ran while one was open for 5% -> 0% of each run, Pallas kernels for 0% -> 0%
where the time goes in v1:
time: 283 us; the launch traced here: 282 us
  Pallas kernels  257 us (91%)
  local copies, waits for them, and re-layouts  10.8 us (4%)
  matrix products  7.86 us (3%)
  other arithmetic  5.35 us (2%)
    pallas_call x1, Pallas kernels, experts(): pl.pallas_call(expert_kernel, out_shape=[jax.ShapeDtypeStruct(slots.shape...  108 us
    pallas_call x1, Pallas kernels, unpack(): pl.pallas_call(unpack_kernel, out_shape=jax.ShapeDtypeStruct(cache.shape,...  65.4 us
    pallas_call x1, Pallas kernels, pack(): pl.pallas_call(pack_kernel, out_shape=jax.ShapeDtypeStruct((BEAM - 1, PAG...  56.3 us
    pallas_call x1, Pallas kernels, ask(): pl.pallas_call(ask_kernel, out_shape=shapes, in_specs=[ANY] * 3, out_spec...  14.3 us
    pallas_call x1, Pallas kernels, answer(): pl.pallas_call(answer_kernel, out_shape=shapes, in_specs=[ANY] * 3, out_s...  13 us
    unnamed x31, local copies, waits for them, and re-layouts  5.68 us

profile of v1, /device:TPU:0, one launch (start us, length us, event | category | flops | bytes accessed | tf_op | source)
XLA Modules:
  0.0 282.4 jit_solution(14734869076091041080)
XLA Ops:
  0.6 0.7 dynamic_slice.3
  1.4 0.1 iota_compare_fusion.3
  1.5 14.3 %ask.1 = (bf16[4,32,2048]{2,1,0:T(8,128)(2,1)}, bf16[4,8,2048]{2,1,0:T(8,128)(2,1)}, s32[4,1,32]{2,1,0:T(1,128)}) custom-call(bf16[32,2048]{1,0:T(8,128)(2,1)} %query.1, bf16[4,8,2048]{2,1,0:T(8,128)(2,1)} %bitcast.95, s32[1,32]{1,0:T(1,128)} %bitcast.97), custom_call_target="tpu_custom_call" | custom-call | tf_op jit(solution)/shard_map/ask/pallas_call | solution.py:90
  15.8 1.1 copy.71
  16.9 2.2 select_reduce_fusion.1
  19.1 0.0 copy-start.1
  19.1 2.1 fusion.30
  21.2 1.1 copy.54
  22.4 0.1 copy.56
  22.4 0.3 copy.55
  22.8 0.6 pad.4.stats
  23.4 0.0 copy-done.1
  23.4 3.1 %fusion.9 = bf16[4,32,16,128]{3,0,2,1:T(4,128)(2,1)S(1)} fusion(bf16[32,8,4096]{2,1,0:T(8,128)(2,1)S(1)} %copy-done.1, f32[4,32,16,8]{3,0,2,1:T(4,128)S(1)} %get-tuple-element.25, f32[4,32,16]{0,2,1:T(8,128)} %fusion.30, f32[4,32,16]{0,2,1:T(8,128)S(1)} %get-tuple-element.24, pred[32,8]{1,0:T(8,128)(4,1)S(1)} %iota_compare_fusion.3), kind=kOutput, calls=%fused_computation.15 | convolution fusion | flops 4521984 | bytes 2895872 | tf_op jit(solution)/shard_map/brhp,rphk->brhk/dot_general | solution.py:512
  26.5 0.1 copy.53
  26.6 1.0 reshape.145.outs
  27.6 0.0 copy-start.5
  27.6 2.8 slice_bitcast_fusion.1
  30.4 0.0 copy-start.12
  30.4 0.0 copy-done.5
  30.4 1.2 fusion.14
  31.6 0.0 copy-done.12
  31.6 0.1 iota_compare_fusion.4
  31.6 0.4 fusion.60
  32.0 0.0 copy-start.10
  32.0 0.0 copy-start.4
  32.0 0.0 copy-start.3
  32.1 0.7 fusion.23
  32.8 0.0 copy-start.6
  32.8 0.7 copy.103
  33.5 13.0 %answer.1 = (bf16[4,32,2048]{2,1,0:T(8,128)(2,1)}, f32[4,32,128]{2,1,0:T(8,128)}, bf16[4,8,2048]{2,1,0:T(8,128)(2,1)}) custom-call(bf16[4,32,2048]{2,1,0:T(8,128)(2,1)} %reshape.145.outs, f32[4,32,128]{2,1,0:T(8,128)} %pad.4.stats, bf16[4,8,2048]{2,1,0:T(8,128)(2,1)} %bitcast.93), custom_call_target="tpu_custom_call" | custom-call | tf_op jit(solution)/shard_map/answer/pallas_call | solution.py:149
  46.5 0.0 copy-start.2
  46.5 0.0 copy-start.7
  46.5 0.0 copy-done.10
  46.5 1.0 select_reduce_fusion.3
  47.5 0.0 copy-done.4
  47.6 0.0 copy-start.8
  47.6 0.0 copy-start.9
  47.6 0.0 copy-done.3
  47.7 0.1 fusion.41
  47.8 0.1 mul.91
  48.0 0.1 mul.94
  48.1 0.0 copy-done.2
  48.1 0.2 select_reduce_fusion
  48.3 0.0 copy-done.6
  48.3 0.0 copy-done.7
  48.3 0.3 fusion.58
  48.7 0.2 multiply_reduce_fusion
  48.9 0.0 copy-done.8
  48.9 0.1 copy.61
  49.0 0.1 reduce_window_sum.11
  49.0 0.1 copy.63
  49.1 0.1 fusion.49
  49.2 0.0 copy-done.9
  49.2 0.3 fusion.1.slots
  49.6 56.3 %pack.1.pages = bf16[3,16,8,4096]{3,2,1,0:T(8,128)(2,1)} custom-call(s32[4,32]{1,0:T(4,128)} %bitcast.96, bf16[32,8,4096]{2,1,0:T(8,128)(2,1)} %cache.3), custom_call_target="tpu_custom_call" | custom-call | tf_op jit(solution)/shard_map/pack/pallas_call | solution.py:183
  105.9 108.4 %experts.1 = (bf16[16,8,2048]{2,1,0:T(8,128)(2,1)S(1)}, bf16[3,16,8,4096]{3,2,1,0:T(8,128)(2,1)S(1)}) custom-call(bf16[16,8,2048]{2,1,0:T(8,128)(2,1)S(1)} %fusion.1.slots, bf16[2048,1024]{1,0:T(8,128)(2,1)} %bitcast.84, bf16[1024,2048]{1,0:T(8,128)(2,1)} %bitcast.85, bf16[3,16,8,4096]{3,2,1,0:T(8,128)(2,1)} %pack.1.pages), custom_call_target="tpu_custom_call" | custom-call | tf_op jit(solution)/shard_map/experts/pallas_call | solution.py:457
  214.2 0.0 copy-start
  214.3 1.7 copy-done
  215.9 0.0 copy-start.11
  215.9 65.4 %unpack.1 = bf16[32,8,4096]{2,1,0:T(8,128)(2,1)} custom-call(s32[32]{0:T(128)} %parents.1, bf16[32,8,4096]{2,1,0:T(8,128)(2,1)} %cache.3, bf16[3,16,8,4096]{3,2,1,0:T(8,128)(2,1)} %copy-done), custom_call_target="tpu_custom_call" | custom-call | tf_op jit(solution)/shard_map/unpack/pallas_call | solution.py:221
  281.4 0.0 copy-done.11
  281.4 0.3 fusion.10
  281.7 0.7 add_convert_fusion
  (13 shorter events, 0.2 us)
Async XLA Ops:
  19.1 4.2 %copy-start.1 = (bf16[32,8,4096]{2,1,0:T(8,128)(2,1)S(1)}, bf16[32,8,4096]{2,1,0:T(8,128)(2,1)}, u32[]{:S(2)}) copy-start(bf16[32,8,4096]{2,1,0:T(8,128)(2,1)} %cache.3) | copy-start | bytes 6291460
  27.6 2.8 copy-start.5
  30.4 1.2 copy-start.12
  32.0 14.5 %copy-start.10 = (s32[32]{0:T(128)S(1)}, s32[32]{0:T(128)}, u32[]{:S(2)}) copy-start(s32[32]{0:T(128)} %parents.1) | copy-start | bytes 388
  32.0 15.5 %copy-start.4 = (bf16[32,4096]{1,0:T(8,128)(2,1)S(1)}, bf16[32,4096]{1,0:T(8,128)(2,1)}, u32[]{:S(2)}) copy-start(bf16[32,4096]{1,0:T(8,128)(2,1)} %param.16) | copy-start | bytes 786436
  32.0 15.6 %copy-start.3 = (bf16[32,2048]{1,0:T(8,128)(2,1)S(1)}, bf16[32,2048]{1,0:T(8,128)(2,1)}, u32[]{:S(2)}) copy-start(bf16[32,2048]{1,0:T(8,128)(2,1)} %query.1) | copy-start | bytes 393220
  32.8 15.5 %copy-start.6 = (bf16[32,2048]{1,0:T(8,128)(2,1)S(1)}, bf16[32,2048]{1,0:T(8,128)(2,1)}, u32[]{:S(2)}) copy-start(bf16[32,2048]{1,0:T(8,128)(2,1)} %param.14) | copy-start | bytes 393220
  46.5 1.6 copy-start.2
  46.5 1.8 copy-start.7
  47.6 1.3 copy-start.8
  47.6 1.6 copy-start.9
  214.2 1.7 copy-start
  215.9 65.5 %copy-start.11 = (f32[32,2]{0,1:T(2,128)S(1)}, f32[32,2]{0,1:T(2,128)}, u32[]{:S(2)}) copy-start(f32[32,2]{0,1:T(2,128)} %param.25) | copy-start | bytes 772

commit v2 on v1

--- a/solution.py
+++ b/solution.py
@@ -184,8 +184,9 @@
         pack_kernel,
         out_shape=jax.ShapeDtypeStruct((BEAM - 1, PAGE_CAP) + cache.shape[1:], cache.dtype),
         in_specs=[pl.BlockSpec(memory_space=pltpu.SMEM), ANY],
-        out_specs=ANY,
+        out_specs=pl.BlockSpec(memory_space=pltpu.VMEM),
         scratch_shapes=[DMA((BEAM - 1, cache.shape[0]))],
+        compiler_params=pltpu.CompilerParams(vmem_limit_bytes=32 * 2**20),
         name="pack",
     )(wishes, cache)
 
@@ -222,8 +223,9 @@
         unpack_kernel,
         out_shape=jax.ShapeDtypeStruct(cache.shape, cache.dtype),
         in_specs=[pl.BlockSpec(memory_space=pltpu.SMEM), ANY, ANY],
-        out_specs=ANY,
+        out_specs=pl.BlockSpec(memory_space=pltpu.VMEM),
         scratch_shapes=[DMA],
+        compiler_params=pltpu.CompilerParams(vmem_limit_bytes=32 * 2**20),
         name="unpack",
     )(parents, cache, arrived)
 
@@ -234,10 +236,10 @@
 
 def expert_kernel(
     slots, first, second, pages, returned, arrived,
-    held, first_v, second_v, picked, inner, total, to_twin, from_twin, to_chip, from_chip, result,
+    held, first_v, second_v, picked, inner, total, to_twin, from_twin, to_chip, from_chip, far, result,
     w_sem, local, d_send, d_recv, r_send, r_recv,
     g_send, g_recv, o_send, o_recv, t_send, t_recv,
-    y_send, y_recv, x_send, x_recv, p_send, p_recv,
+    y_send, y_recv, x_send, x_recv, f_send, f_recv, p_send, p_recv,
 ):
     dp, ex, z, y = place()
     x, core = lax.div(dp, 2), lax.rem(dp, 2)
@@ -319,11 +321,15 @@
         move.start()
         paged.append(move)
 
-    def project(which):
-        cells = picked.shape[0] // 2
+    cells = picked.shape[0] // 2
+    tile = min(1024, hidden)
+    wide = min(1024, width)
+    slim = min(256, width)
+    band = block // 4
+
+    def up(which):
         for half, owner in ((0, core), (1, 1 - core)):
             picked[half * cells : (half + 1) * cells, :] = held[chip[which], owner].reshape(cells, width)
-        tile = min(256, hidden)
 
         @pl.loop(0, hidden // tile)
         def _(n):
@@ -331,8 +337,7 @@
             part = jnp.dot(picked[...], first_v[:, spot], preferred_element_type=jnp.float32)
             inner[:, spot] = jnp.maximum(part, 0.0).astype(inner.dtype)
 
-        wide = min(256, width)
-
+    def down(which):
         @pl.loop(0, width // wide)
         def _(n):
             spot = pl.ds(pl.multiple_of(n * wide, wide), wide)
@@ -347,20 +352,44 @@
     def forward(which):
         there = from_twin.at[which]
         send(there, there, y_send.at[which], y_recv.at[which], twin, ex).wait_recv()
-        wide = min(256, width)
-
-        @pl.loop(0, width // wide)
+
+        @pl.loop(0, width // slim)
         def _(n):
-            spot = pl.ds(pl.multiple_of(n * wide, wide), wide)
+            spot = pl.ds(pl.multiple_of(n * slim, slim), slim)
             both = total[which, :, spot] + from_twin[which, :, spot].astype(jnp.float32)
             to_chip[which - 1, :, spot] = both.astype(to_chip.dtype)
 
-        move = send(
-            to_chip.at[which - 1], from_chip.at[which - 1], x_send.at[which - 1], x_recv.at[which - 1],
-            chip[which] * 2 + core, ex,
-        )
+        if which == OPPOSITE:
+            for q in (0, 2, 1, 3):
+                rows = pl.ds(q * band, band)
+                relay(to_chip.at[2, rows], far.at[rows], f_send.at[q], f_recv.at[q], RIGHT if q < 2 else LEFT)
+        else:
+            for q in (2, 3) if which == RIGHT else (0, 1):
+                last_leg(which, q)
+
+    def relay(src, dst, send_sem, recv_sem, side):
+        move = send(src, dst, send_sem, recv_sem, chip[side] * 2 + core, ex)
         move.start()
         sent.append(move)
+
+    def last_leg(which, q):
+        rows = pl.ds(q * band, band)
+        spot = which - 1
+        relay(to_chip.at[spot, rows], from_chip.at[spot, rows], x_send.at[spot, q], x_recv.at[spot, q], which)
+
+    def merge(q):
+        rows = pl.ds(q * band, band)
+        which = RIGHT if q < 2 else LEFT
+        there = far.at[rows]
+        send(there, there, f_send.at[q], f_recv.at[q], dp, ex).wait_recv()
+
+        @pl.loop(0, width // slim)
+        def _(n):
+            spot = pl.ds(pl.multiple_of(n * slim, slim), slim)
+            both = to_chip[which - 1, rows, spot].astype(jnp.float32) + far[rows, spot].astype(jnp.float32)
+            to_chip[which - 1, rows, spot] = both.astype(to_chip.dtype)
+
+        last_leg(which, q)
 
     def landed(way, j):
         side = LEFT if way == 0 else RIGHT
@@ -376,55 +405,58 @@
     for load in loads:
         load.wait()
     from_sibling(OWN)
-    project(OWN)
+    up(OWN)
+    down(OWN)
     for j in range(4):
         landed(0, j)
         landed(1, j)
     from_sibling(LEFT)
-    project(LEFT)
+    up(LEFT)
+    down(LEFT)
     from_sibling(RIGHT)
-    project(RIGHT)
+    up(RIGHT)
     forward(LEFT)
-    forward(RIGHT)
+    down(RIGHT)
     for j in range(4):
         part = chunk(OPPOSITE, core, j)
         send(part, part, o_send.at[j], o_recv.at[j], dp, ex).wait_recv()
         to_sibling(OPPOSITE, j)
     from_sibling(OPPOSITE)
-    project(OPPOSITE)
+    up(OPPOSITE)
+    forward(RIGHT)
+    down(OPPOSITE)
     forward(OPPOSITE)
+    for q in (0, 2, 1, 3):
+        merge(q)
 
     there = from_twin.at[OWN]
     send(there, there, y_send.at[OWN], y_recv.at[OWN], twin, ex).wait_recv()
-    for which in (LEFT, RIGHT, OPPOSITE):
-        there = from_chip.at[which - 1]
-        send(there, there, x_send.at[which - 1], x_recv.at[which - 1], dp, ex).wait_recv()
-    wide = min(256, width)
-
-    @pl.loop(0, width // wide)
-    def _(n):
-        spot = pl.ds(pl.multiple_of(n * wide, wide), wide)
-        whole = total[OWN, :, spot] + from_twin[OWN, :, spot].astype(jnp.float32)
-        for which in (LEFT, RIGHT, OPPOSITE):
-            whole = whole + from_chip[which - 1, :, spot].astype(jnp.float32)
-        result[:, :, spot] = whole.astype(result.dtype).reshape(EXPERTS, block // EXPERTS, wide)
-
+    cap = block // EXPERTS
     stay = pltpu.make_async_copy(result.at[ex], returned.at[ex], local.at[1])
-    stay.start()
-    for a in (2, 1, 3, 0):
-        for b in range(GROUP):
-            if a or b:
-                spot = a * GROUP + b
-                move = send(result.at[peer(a, b)], returned.at[ex], r_send.at[spot], r_recv.at[spot], dp, peer(a, b))
-                move.start()
-                sent.append(move)
+    for q in (0, 2, 1, 3):
+        rows = pl.ds(q * band, band)
+        for spot in (0, 1):
+            there = from_chip.at[spot, rows]
+            send(there, there, x_send.at[spot, q], x_recv.at[spot, q], dp, ex).wait_recv()
+
+        @pl.loop(0, width // slim)
+        def _(n):
+            spot = pl.ds(pl.multiple_of(n * slim, slim), slim)
+            whole = total[OWN, rows, spot] + from_twin[OWN, rows, spot].astype(jnp.float32)
+            for side in (0, 1):
+                whole = whole + from_chip[side, rows, spot].astype(jnp.float32)
+            packets = whole.astype(result.dtype).reshape(GROUP, cap, slim)
+            result[q * GROUP : (q + 1) * GROUP, :, spot] = packets
+
+        for target in range(q * GROUP, (q + 1) * GROUP):
+            move = send(result.at[target], returned.at[ex], r_send.at[target], r_recv.at[ex], dp, target)
+            pl.when(target != ex)(move.start)
+            pl.when(target == ex)(stay.start)
+    for origin in range(EXPERTS):
+        there = returned.at[origin]
+        move = send(there, there, r_send.at[origin], r_recv.at[origin], dp, origin)
+        pl.when(origin != ex)(move.wait)
     stay.wait()
-    for a in range(BEAM):
-        for b in range(GROUP):
-            if a or b:
-                spot = a * GROUP + b
-                there = returned.at[source(a, b)]
-                send(there, there, r_send.at[spot], r_recv.at[spot], dp, source(a, b)).wait_recv()
     for move in sent:
         move.wait_send()
     for move in paged:
@@ -446,13 +478,14 @@
         pltpu.VMEM((4, block, width), kind),
         pltpu.VMEM((4, block, width), kind),
         pltpu.VMEM((3, block, width), kind),
-        pltpu.VMEM((3, block, width), kind),
+        pltpu.VMEM((2, block, width), kind),
+        pltpu.VMEM((block, width), kind),
         pltpu.VMEM((count, cap, width), kind),
     ]
     sems = [
         DMA((2,)), DMA((2,)), DMA((16,)), DMA((16,)), DMA((16,)), DMA((16,)),
         DMA((2, 4)), DMA((2, 4)), DMA((4,)), DMA((4,)), DMA((4, 4)), DMA((4, 4)),
-        DMA((4,)), DMA((4,)), DMA((3,)), DMA((3,)), DMA((3,)), DMA((3,)),
+        DMA((4,)), DMA((4,)), DMA((2, 4)), DMA((2, 4)), DMA((4,)), DMA((4,)), DMA((3,)), DMA((3,)),
     ]
     return pl.pallas_call(
         expert_kernel,

time: 283 us -> 135 us (0.48)
  Pallas kernels: 257 us -> 110 us
    pallas_call x1, Pallas kernels: 65.4 us -> 5.64 us  [unpack(): pl.pallas_call(unpack_kernel, out_shape=jax.ShapeDtypeStruct(cache.shape,...]
    pallas_call x1, Pallas kernels: 56.3 us -> 5.6 us  [pack(): pl.pallas_call(pack_kernel, out_shape=jax.ShapeDtypeStruct((BEAM - 1, PAG...]
    pallas_call x1, Pallas kernels: 108 us -> 71.3 us  [experts(): pl.pallas_call(expert_kernel, out_shape=[jax.ShapeDtypeStruct(slots.shape...]
    unnamed x31 -> x33, local copies, waits for them, and re-layouts: 5.68 us -> 5.69 us
where the time goes in v2:
time: 135 us
  Pallas kernels  110 us (81%)
  local copies, waits for them, and re-layouts  10.8 us (8%)
  matrix products  7.85 us (6%)
  other arithmetic  5.36 us (4%)
    pallas_call x1, Pallas kernels, experts(): pl.pallas_call(expert_kernel, out_shape=[jax.ShapeDtypeStruct(slots.shape...  71.3 us
    pallas_call x1, Pallas kernels, ask(): pl.pallas_call(ask_kernel, out_shape=shapes, in_specs=[ANY] * 3, out_spec...  14.3 us
    pallas_call x1, Pallas kernels, answer(): pl.pallas_call(answer_kernel, out_shape=shapes, in_specs=[ANY] * 3, out_s...  13 us
    unnamed x33, local copies, waits for them, and re-layouts  5.69 us
    pallas_call x1, Pallas kernels, unpack(): pl.pallas_call(unpack_kernel, out_shape=jax.ShapeDtypeStruct(cache.shape,...  5.64 us
    pallas_call x1, Pallas kernels, pack(): pl.pallas_call(pack_kernel, out_shape=jax.ShapeDtypeStruct((BEAM - 1, PAG...  5.6 us
    dot_general x1, matrix products, per_device(): jnp.einsum('brhp,rphk->brhk', weights, values, preferred_element_type=jnp...  3.11 us

profile of v2, /device:TPU:0, one launch (start us, length us, event | category | flops | bytes accessed | tf_op | source)
XLA Modules:
  0.0 134.9 jit_solution(13619141208335193587)
XLA Ops:
  0.6 0.7 dynamic_slice.3
  1.4 0.1 iota_compare_fusion.3
  1.5 14.3 %ask.1 = (bf16[4,32,2048]{2,1,0:T(8,128)(2,1)}, bf16[4,8,2048]{2,1,0:T(8,128)(2,1)}, s32[4,1,32]{2,1,0:T(1,128)}) custom-call(bf16[32,2048]{1,0:T(8,128)(2,1)} %query.1, bf16[4,8,2048]{2,1,0:T(8,128)(2,1)} %bitcast.97, s32[1,32]{1,0:T(1,128)} %bitcast.85), custom_call_target="tpu_custom_call" | custom-call | tf_op jit(solution)/shard_map/ask/pallas_call | solution.py:90
  15.8 1.1 copy.71
  16.9 2.2 %select_reduce_fusion.1 = (f32[4,32,16]{0,2,1:T(8,128)S(1)}, f32[4,32,16,8]{3,0,2,1:T(4,128)S(1)}) fusion(pred[32,8]{1,0:T(8,128)(4,1)S(1)} %iota_compare_fusion.3, bf16[32,8,4096]{2,1,0:T(8,128)(2,1)} %cache.3, bf16[4,32,16,128]{3,2,1,0:T(8,128)(2,1)S(1)} %bitcast.91), kind=kOutput, calls=%fused_computation.29 | convolution fusion | flops 4241408 | bytes 1646848 | tf_op jit(solution)/shard_map/brhk,rphk->brhp/dot_general | solution.py:540
  19.1 0.0 copy-start.1
  19.1 2.1 %fusion.30 = f32[4,32,16]{0,2,1:T(8,128)} fusion(f32[4,32,16,8]{3,0,2,1:T(4,128)S(1)} %get-tuple-element.25, f32[4,32,16]{0,2,1:T(8,128)S(1)} %get-tuple-element.24, pred[32,8]{1,0:T(8,128)(4,1)S(1)} %iota_compare_fusion.3), kind=kLoop, calls=%fused_computation.32 | loop fusion | flops 47104 | bytes 82176 | tf_op jit(solution)/shard_map/reduce_sum | solution.py:543
  21.2 1.1 copy.54
  22.4 0.1 copy.56
  22.4 0.3 copy.55
  22.8 0.6 pad.4.stats
  23.4 0.0 copy-done.1
  23.4 3.1 %fusion.9 = bf16[4,32,16,128]{3,0,2,1:T(4,128)(2,1)S(1)} fusion(bf16[32,8,4096]{2,1,0:T(8,128)(2,1)S(1)} %copy-done.1, f32[4,32,16,8]{3,0,2,1:T(4,128)S(1)} %get-tuple-element.25, f32[4,32,16]{0,2,1:T(8,128)} %fusion.30, f32[4,32,16]{0,2,1:T(8,128)S(1)} %get-tuple-element.24, pred[32,8]{1,0:T(8,128)(4,1)S(1)} %iota_compare_fusion.3), kind=kOutput, calls=%fused_computation.15 | convolution fusion | flops 4521984 | bytes 2895872 | tf_op jit(solution)/shard_map/brhp,rphk->brhk/dot_general | solution.py:545
  26.5 0.1 copy.53
  26.6 1.0 reshape.145.outs
  27.6 0.0 copy-start.7
  27.6 2.8 %slice_bitcast_fusion.1 = (bf16[8,8,16,8,128]{4,3,2,1,0:T(8,128)(2,1)S(1)}, bf16[8,8,16,8,128]{4,3,2,1,0:T(8,128)(2,1)S(1)}) fusion(bf16[8,64,4096]{2,1,0:T(8,128)(2,1)} %param.21), kind=kLoop, calls=%fused_computation.11 | loop fusion | bytes 8388608
  30.4 0.0 copy-start.13
  30.4 0.0 copy-done.7
  30.4 1.2 fusion.14
  31.6 0.0 copy-done.13
  31.6 0.1 iota_compare_fusion.4
  31.6 0.4 fusion.60
  32.0 0.0 copy-start.3
  32.0 0.0 copy-start.6
  32.0 0.0 copy-start.5
  32.1 0.7 fusion.23
  32.8 0.7 copy.103
  33.5 13.0 %answer.1 = (bf16[4,32,2048]{2,1,0:T(8,128)(2,1)}, f32[4,32,128]{2,1,0:T(8,128)}, bf16[4,8,2048]{2,1,0:T(8,128)(2,1)}) custom-call(bf16[4,32,2048]{2,1,0:T(8,128)(2,1)} %reshape.145.outs, f32[4,32,128]{2,1,0:T(8,128)} %pad.4.stats, bf16[4,8,2048]{2,1,0:T(8,128)(2,1)} %bitcast.95), custom_call_target="tpu_custom_call" | custom-call | tf_op jit(solution)/shard_map/answer/pallas_call | solution.py:149
  46.5 0.0 copy-start.4
  46.5 0.0 copy-start.9
  46.5 0.0 copy-done.3
  46.5 1.0 select_reduce_fusion.3
  47.5 0.0 copy-done.6
  47.5 0.0 copy-start.10
  47.6 0.0 copy-start.11
  47.6 0.0 copy-done.5
  47.7 0.1 fusion.41
  47.8 0.0 copy-start.2
  47.8 0.1 mul.91
  48.0 0.1 mul.94
  48.1 0.0 copy-done.4
  48.1 0.2 select_reduce_fusion
  48.3 0.0 copy-done.8
  48.3 0.0 copy-done.9
  48.3 0.3 fusion.58
  48.7 0.2 multiply_reduce_fusion
  48.9 0.0 copy-done.10
  48.9 0.1 copy.61
  49.0 0.1 reduce_window_sum.11
  49.0 0.1 copy.63
  49.1 0.1 fusion.49
  49.2 0.0 copy-done.11
  49.2 0.3 fusion.1.slots
  49.6 0.0 copy-done.2
  49.6 5.6 %pack.1.pages = bf16[3,16,8,4096]{3,2,1,0:T(8,128)(2,1)S(1)} custom-call(s32[4,32]{1,0:T(4,128)S(1)} %bitcast.84, bf16[32,8,4096]{2,1,0:T(8,128)(2,1)S(1)} %copy-done.1), custom_call_target="tpu_custom_call" | custom-call | tf_op jit(solution)/shard_map/pack/pallas_call | solution.py:183
  55.2 0.0 copy-start
  55.2 1.7 %copy-done = bf16[3,16,8,4096]{3,2,1,0:T(8,128)(2,1)} copy-done((bf16[3,16,8,4096]{3,2,1,0:T(8,128)(2,1)}, bf16[3,16,8,4096]{3,2,1,0:T(8,128)(2,1)S(1)}, u32[]{:S(2)}) %copy-start) | copy-done | bytes 3145752
  56.9 71.3 %experts.1 = (bf16[16,8,2048]{2,1,0:T(8,128)(2,1)S(1)}, bf16[3,16,8,4096]{3,2,1,0:T(8,128)(2,1)S(1)}) custom-call(bf16[16,8,2048]{2,1,0:T(8,128)(2,1)S(1)} %fusion.1.slots, bf16[2048,1024]{1,0:T(8,128)(2,1)} %bitcast.86, bf16[1024,2048]{1,0:T(8,128)(2,1)} %bitcast.87, bf16[3,16,8,4096]{3,2,1,0:T(8,128)(2,1)} %copy-done), custom_call_target="tpu_custom_call" | custom-call | tf_op jit(solution)/shard_map/experts/pallas_call | solution.py:490
  128.2 0.0 copy-start.12
  128.2 5.6 %unpack.1 = bf16[32,8,4096]{2,1,0:T(8,128)(2,1)} custom-call(s32[32]{0:T(128)S(1)} %copy-done.3, bf16[32,8,4096]{2,1,0:T(8,128)(2,1)S(1)} %copy-done.1, bf16[3,16,8,4096]{3,2,1,0:T(8,128)(2,1)S(1)} %get-tuple-element.17.arrived), custom_call_target="tpu_custom_call" | custom-call | tf_op jit(solution)/shard_map/unpack/pallas_call | solution.py:222
  133.9 0.0 copy-done.12
  133.9 0.3 fusion.10
  134.2 0.7 add_convert_fusion
  (14 shorter events, 0.2 us)
Async XLA Ops:
  19.1 4.2 %copy-start.1 = (bf16[32,8,4096]{2,1,0:T(8,128)(2,1)S(1)}, bf16[32,8,4096]{2,1,0:T(8,128)(2,1)}, u32[]{:S(2)}) copy-start(bf16[32,8,4096]{2,1,0:T(8,128)(2,1)} %cache.3) | copy-start | bytes 6291460
  27.6 2.8 %copy-start.7 = (bf16[4,8,2048]{2,1,0:T(8,128)(2,1)S(1)}, bf16[4,8,2048]{2,1,0:T(8,128)(2,1)}, u32[]{:S(2)}) copy-start(bf16[4,8,2048]{2,1,0:T(8,128)(2,1)} %get-tuple-element.11) | copy-start | bytes 393220
  30.4 1.2 copy-start.13
  32.0 14.5 %copy-start.3 = (s32[32]{0:T(128)S(1)}, s32[32]{0:T(128)}, u32[]{:S(2)}) copy-start(s32[32]{0:T(128)} %parents.1) | copy-start | bytes 388
  32.0 15.5 %copy-start.6 = (bf16[32,4096]{1,0:T(8,128)(2,1)S(1)}, bf16[32,4096]{1,0:T(8,128)(2,1)}, u32[]{:S(2)}) copy-start(bf16[32,4096]{1,0:T(8,128)(2,1)} %param.16) | copy-start | bytes 786436
  32.0 15.6 %copy-start.5 = (bf16[32,2048]{1,0:T(8,128)(2,1)S(1)}, bf16[32,2048]{1,0:T(8,128)(2,1)}, u32[]{:S(2)}) copy-start(bf16[32,2048]{1,0:T(8,128)(2,1)} %query.1) | copy-start | bytes 393220
  32.8 15.5 %copy-start.8 = (bf16[32,2048]{1,0:T(8,128)(2,1)S(1)}, bf16[32,2048]{1,0:T(8,128)(2,1)}, u32[]{:S(2)}) copy-start(bf16[32,2048]{1,0:T(8,128)(2,1)} %param.14) | copy-start | bytes 393220
  46.5 1.6 %copy-start.4 = (bf16[4,32,2048]{2,1,0:T(8,128)(2,1)S(1)}, bf16[4,32,2048]{2,1,0:T(8,128)(2,1)}, u32[]{:S(2)}) copy-start(bf16[4,32,2048]{2,1,0:T(8,128)(2,1)} %get-tuple-element.13) | copy-start | bytes 1572868
  46.5 1.8 %copy-start.9 = (bf16[4,8,2048]{2,1,0:T(8,128)(2,1)S(1)}, bf16[4,8,2048]{2,1,0:T(8,128)(2,1)}, u32[]{:S(2)}) copy-start(bf16[4,8,2048]{2,1,0:T(8,128)(2,1)} %get-tuple-element.14) | copy-start | bytes 393220
  47.5 1.3 copy-start.10
  47.6 1.7 %copy-start.11 = (f32[2048]{0:T(1024)S(1)}, f32[2048]{0:T(1024)}, u32[]{:S(2)}) copy-start(f32[2048]{0:T(1024)} %param.23) | copy-start | bytes 24580
  47.8 1.8 %copy-start.2 = (s32[4,1,32]{2,1,0:T(1,128)S(1)}, s32[4,1,32]{2,1,0:T(1,128)}, u32[]{:S(2)}) copy-start(s32[4,1,32]{2,1,0:T(1,128)} %get-tuple-element.15) | copy-start | bytes 1540
  55.2 1.7 %copy-start = (bf16[3,16,8,4096]{3,2,1,0:T(8,128)(2,1)}, bf16[3,16,8,4096]{3,2,1,0:T(8,128)(2,1)S(1)}, u32[]{:S(2)}) copy-start(bf16[3,16,8,4096]{3,2,1,0:T(8,128)(2,1)S(1)} %pack.1.pages) | copy-start | bytes 9437188
  128.2 5.7 %copy-start.12 = (f32[32,2]{0,1:T(2,128)S(1)}, f32[32,2]{0,1:T(2,128)}, u32[]{:S(2)}) copy-start(f32[32,2]{0,1:T(2,128)} %param.25) | copy-start | bytes 772

commit v3 on v2

v3 whole, which is shorter than its diff:
```python
import functools
import math

import jax
import jax.numpy as jnp
from jax import lax
from jax.experimental import pallas as pl
from jax.experimental.pallas import tpu as pltpu
from jax.sharding import PartitionSpec as P

HEAD = 128
BEAM = 4
GROUP = 4
CHIPS = 4
EXPERTS = 16
PAGE_CAP = 16
MESH = pl.DeviceIdType.MESH
ANY = pl.BlockSpec(memory_space=pl.ANY)
DMA = pltpu.SemaphoreType.DMA


def place():
    dp = lax.axis_index("dp")
    ex = lax.axis_index("expert")
    return dp, ex, lax.div(ex, GROUP), lax.rem(ex, GROUP)


def send(src, dst, send_sem, recv_sem, dp, ex):
    return pltpu.make_async_remote_copy(
        src_ref=src,
        dst_ref=dst,
        send_sem=send_sem,
        recv_sem=recv_sem,
        device_id=(dp, ex),
        device_id_type=MESH,
    )


def greet(barrier, dp, ex):
    pl.semaphore_signal(barrier, inc=1, device_id=(dp, ex), device_id_type=MESH)


def unpack_kernel(parents, cache, arrived, fresh, sem):
    _, _, z, _ = place()
    rows = cache.shape[0]

    def begin(row, counts):
        parent = parents[row]
        off = lax.rem(z - parent + BEAM, BEAM)

        def keep():
            pltpu.make_async_copy(cache.at[row], fresh.at[row], sem).start()

        pl.when(off == 0)(keep)
        after = []
        for step in range(1, BEAM):
            hit = off == step

            def take(step=step):
                pltpu.make_async_copy(arrived.at[step - 1, counts[step - 1]], fresh.at[row], sem).start()

            pl.when(hit)(take)
            after.append(counts[step - 1] + hit.astype(jnp.int32))
        return tuple(after)

    lax.fori_loop(0, rows, begin, (jnp.int32(0),) * (BEAM - 1))
    pltpu.make_async_copy(cache, fresh, sem).wait()


def unpack(parents, cache, arrived):
    return pl.pallas_call(
        unpack_kernel,
        out_shape=jax.ShapeDtypeStruct(cache.shape, cache.dtype),
        in_specs=[pl.BlockSpec(memory_space=pltpu.SMEM), ANY, ANY],
        out_specs=pl.BlockSpec(memory_space=pltpu.VMEM),
        scratch_shapes=[DMA],
        compiler_params=pltpu.CompilerParams(vmem_limit_bytes=58 * 2**20),
        name="unpack",
    )(parents, cache, arrived)


ORDER = (0, 1, 3, 2)
OWN, LEFT, RIGHT, OPPOSITE = range(4)


def layer_kernel(
    query, cross, lanes, info, tokens, new_kv, gain, cache, memory, first, second,
    mixed, arrived,
    cache_v, memory_v, tokens_v, new_kv_v, gain_v, info_v, queries, wishes, crosses,
    outs, stats, owner_out, got, got_stats, cross_out, hidden_v, pages, slots, returned,
    held, first_v, second_v, picked, inner, total, to_twin, from_twin, to_chip, from_chip, far, result,
    l_sem, local, k_send, k_recv, n_send, n_recv, e_send, e_recv, b_send, b_recv, s_send, s_recv, c_send, c_recv,
    d_send, d_recv, r_send, r_recv,
    g_send, g_recv, o_send, o_recv, t_send, t_recv,
    y_send, y_recv, x_send, x_recv, f_send, f_recv, p_send, p_recv,
):
    dp, ex, z, y = place()
    x, core = lax.div(dp, 2), lax.rem(dp, 2)
    twin = x * 2 + 1 - core
    chip = [x, lax.rem(x + CHIPS - 1, CHIPS), lax.rem(x + 1, CHIPS), lax.rem(x + 2, CHIPS)]
    row_count, width = tokens.shape
    hidden = first.shape[-1]
    kind = tokens.dtype
    heads = width // HEAD
    span = cache.shape[1]
    quarter, reach = memory.shape[:2]
    block = EXPERTS * slots.shape[1]
    scale = 1.0 / math.sqrt(HEAD)

    barrier = pltpu.get_barrier_semaphore()
    for a in range(BEAM):
        for b in range(GROUP):
            if a or b:
                greet(barrier, dp, lax.rem(z + a, BEAM) * GROUP + lax.rem(y + b, GROUP))
    greet(barrier, twin, ex)
    for side in (LEFT, RIGHT, OPPOSITE):
        greet(barrier, chip[side] * 2 + core, ex)
    pairs = (
        (first, first_v), (second, second_v), (cache, cache_v), (memory, memory_v), (tokens, tokens_v),
        (new_kv, new_kv_v), (gain, gain_v), (info, info_v), (query, queries.at[z]), (lanes, wishes.at[z]),
    )
    loads = [pltpu.make_async_copy(a, b, l_sem.at[i]) for i, (a, b) in enumerate(pairs)]
    for i in (9, 8, 2, 5, 3, 4, 6, 7, 0, 1):
        loads[i].start()
    own_cross = pltpu.make_async_copy(cross.at[y], crosses.at[z], local.at[2])
    pl.when(z == y)(own_cross.start)
    pl.semaphore_wait(barrier, EXPERTS - 1 + 4)

    sent = []
    asks = []
    for off in (1, 3, 2):
        target = lax.rem(z + off, BEAM) * GROUP + y
        asks.append(send(lanes, wishes.at[z], n_send.at[off - 1], n_recv.at[off - 1], dp, target))
        asks.append(send(query, queries.at[z], k_send.at[off - 1], k_recv.at[off - 1], dp, target))
    for move in asks:
        move.start()
    crossing = [
        send(cross.at[p], crosses.at[z], e_send.at[p], e_recv.at[z], dp, y * GROUP + p) for p in range(GROUP)
    ]
    for p in range(GROUP):
        pl.when(y * GROUP + p != ex)(crossing[p].start)

    for i in (5, 8, 9):
        loads[i].wait()
    lane = lax.broadcasted_iota(jnp.int32, (row_count, HEAD), 1)
    own = jnp.zeros((row_count, HEAD), jnp.float32)
    for h in range(heads):
        spot = slice(h * HEAD, (h + 1) * HEAD)
        both = queries[z, :, spot].astype(jnp.float32) * new_kv_v[:, spot].astype(jnp.float32)
        own = own + jnp.where(lane == h, jnp.sum(both, -1, keepdims=True) * scale, 0.0)

    asked = BEAM * row_count
    shape = (asked, row_count * span)
    lane_row = lax.broadcasted_iota(jnp.int32, shape, 1)
    same = lax.rem(lax.broadcasted_iota(jnp.int32, shape, 0), row_count) == lax.div(lane_row, span)
    loads[2].wait()
    for move in asks:
        move.wait()
    valid = same & (lax.rem(lane_row, span) < wishes[z, 0:1, : shape[1]])
    stat_lane = lax.broadcasted_iota(jnp.int32, (asked, HEAD), 1)
    stats[...] = jnp.zeros_like(stats)

    @pl.loop(0, heads // batch_of(heads))
    def _(n):
        for m in range(batch_of(heads)):
            h = n * batch_of(heads) + m
            spot = pl.ds(pl.multiple_of(h * HEAD, HEAD), HEAD)
            spot_v = pl.ds(pl.multiple_of(width + h * HEAD, HEAD), HEAD)
            q_h = queries[:, :, spot].reshape(asked, HEAD)
            k_h = cache_v[:, :, spot].reshape(row_count * span, HEAD)
            v_h = cache_v[:, :, spot_v].reshape(row_count * span, HEAD)
            scores = lax.dot_general(q_h, k_h, (((1,), (1,)), ((), ())), preferred_element_type=jnp.float32)
            scores = jnp.where(valid, scores * scale, -1e30)
            peak = jnp.max(scores, -1, keepdims=True)
            terms = jnp.exp(scores - peak)
            mass = jnp.sum(terms, -1, keepdims=True)
            part = jnp.dot((terms / mass).astype(kind), v_h, preferred_element_type=jnp.float32)
            outs[:, :, spot] = part.astype(kind).reshape(BEAM, row_count, HEAD)
            level = jnp.where(stat_lane == h, peak + jnp.log(mass), 0.0)
            stats[...] += level.reshape(BEAM, row_count, HEAD)

    answers = []
    for off in (1, 3, 2):
        other = lax.rem(z + off, BEAM)
        target = other * GROUP + y
        answers.append(send(stats.at[other], got_stats.at[z], b_send.at[off - 1], b_recv.at[off - 1], dp, target))
        answers.append(send(outs.at[other], got.at[z], s_send.at[off - 1], s_recv.at[off - 1], dp, target))
    for move in answers:
        move.start()
    stays = [
        pltpu.make_async_copy(outs.at[z], got.at[z], local.at[0]),
        pltpu.make_async_copy(stats.at[z], got_stats.at[z], local.at[1]),
    ]
    for stay in stays:
        stay.start()

    for p in range(GROUP):
        pl.when(y * GROUP + p != ex)(crossing[p].wait_send)
    for beam in range(BEAM):
        coming = send(cross.at[0], crosses.at[beam], e_send.at[0], e_recv.at[beam], dp, beam * GROUP + z)
        pl.when(beam * GROUP + z != ex)(coming.wait_recv)
    pl.when(z == y)(own_cross.wait)
    loads[3].wait()
    asked_c = BEAM * quarter
    shape_c = (asked_c, quarter * reach)
    lane_c = lax.broadcasted_iota(jnp.int32, shape_c, 1)
    same_c = lax.rem(lax.broadcasted_iota(jnp.int32, shape_c, 0), quarter) == lax.div(lane_c, reach)
    valid_c = same_c & (lax.rem(lane_c, reach) < wishes[z, 1:2, : shape_c[1]])

    @pl.loop(0, heads // batch_of(heads))
    def _(n):
        for m in range(batch_of(heads)):
            h = n * batch_of(heads) + m
            spot = pl.ds(pl.multiple_of(h * HEAD, HEAD), HEAD)
            spot_v = pl.ds(pl.multiple_of(width + h * HEAD, HEAD), HEAD)
            q_h = crosses[:, :, spot].reshape(asked_c, HEAD)
            k_h = memory_v[:, :, spot].reshape(quarter * reach, HEAD)
            v_h = memory_v[:, :, spot_v].reshape(quarter * reach, HEAD)
            scores = lax.dot_general(q_h, k_h, (((1,), (1,)), ((), ())), preferred_element_type=jnp.float32)
            scores = jnp.where(valid_c, scores * scale, -1e30)
            peak = jnp.max(scores, -1, keepdims=True)
            terms = jnp.exp(scores - peak)
            mass = jnp.sum(terms, -1, keepdims=True)
            part = jnp.dot((terms / mass).astype(kind), v_h, preferred_element_type=jnp.float32)
            owner_out[:, :, spot] = part.astype(kind).reshape(BEAM, quarter, HEAD)

    own_back = pltpu.make_async_copy(owner_out.at[z], cross_out.at[y], local.at[2])
    crossing = [
        send(owner_out.at[beam], cross_out.at[y], c_send.at[beam], c_recv.at[y], dp, beam * GROUP + z)
        for beam in range(BEAM)
    ]
    for beam in range(BEAM):
        pl.when(beam * GROUP + z != ex)(crossing[beam].start)
    pl.when(z == y)(own_back.start)

    page_shape = (PAGE_CAP * span, row_count * span)
    page_row = lax.broadcasted_iota(jnp.int32, page_shape, 0)
    page_lane = lax.broadcasted_iota(jnp.int32, page_shape, 1)
    page_slot = lax.div(page_row, span)
    same_place = lax.rem(page_row, span) == lax.rem(page_lane, span)
    strip = min(1024, 2 * width)
    for off in (1, 3, 2):
        asker = lax.rem(z + off, BEAM)
        wanted = wishes[asker, 4:5, : page_shape[1]] == z
        pick = same_place & wanted & (page_slot == wishes[asker, 5:6, : page_shape[1]])
        pick = pick.astype(jnp.float32).astype(kind)

        @pl.loop(0, 2 * width // strip)
        def _(n):
            spot = pl.ds(pl.multiple_of(n * strip, strip), strip)
            lines = cache_v[:, :, spot].reshape(row_count * span, strip)
            part = jnp.dot(pick, lines, preferred_element_type=jnp.float32).astype(kind)
            pages[off - 1, :, :, spot] = part.reshape(PAGE_CAP, span, strip)

    for load in loads[4:5] + loads[6:8]:
        load.wait()
    for stay in stays:
        stay.wait()
    for move in answers:
        move.wait()
    for beam in range(BEAM):
        pl.when(beam * GROUP + z != ex)(crossing[beam].wait_send)
    for p in range(GROUP):
        coming = send(owner_out.at[0], cross_out.at[p], c_send.at[0], c_recv.at[p], dp, y * GROUP + p)
        pl.when(y * GROUP + p != ex)(coming.wait_recv)
    pl.when(z == y)(own_back.wait)

    parent = info_v[:, 0:1]
    level = jnp.zeros((row_count, HEAD), jnp.float32)
    for beam in range(BEAM):
        level = level + jnp.where(parent == float(beam), got_stats[beam], 0.0)
    top = jnp.maximum(level, own)
    cache_part = jnp.exp(level - top)
    own_part = jnp.exp(own - top)
    cache_share = cache_part / (cache_part + own_part)
    own_share = own_part / (cache_part + own_part)
    for h in range(heads):
        spot = slice(h * HEAD, (h + 1) * HEAD)
        cached = jnp.zeros((row_count, HEAD), jnp.float32)
        for beam in range(BEAM):
            cached = cached + jnp.where(parent == float(beam), got[beam, :, spot].astype(jnp.float32), 0.0)
        own_value = new_kv_v[:, width + h * HEAD : width + (h + 1) * HEAD].astype(jnp.float32)
        mine = cache_share[:, h : h + 1] * cached + own_share[:, h : h + 1] * own_value
        crossed = cross_out[:, :, spot].reshape(row_count, HEAD).astype(jnp.float32)
        hidden_v[:, spot] = tokens_v[:, spot].astype(jnp.float32) + mine + crossed
    whole = hidden_v[...]
    centered = whole - jnp.mean(whole, -1, keepdims=True)
    variance = jnp.mean(centered * centered, -1, keepdims=True)
    moe_in = (centered * lax.rsqrt(variance + 1e-05) * gain_v[...]).astype(kind)
    slot_row = lax.broadcasted_iota(jnp.int32, (block, row_count), 0)
    table = (slot_row == wishes[z, 2:3, :row_count]) | (slot_row == wishes[z, 3:4, :row_count])
    table = table.astype(jnp.float32).astype(kind)
    packets = jnp.dot(table, moe_in, preferred_element_type=jnp.float32).astype(kind)
    slots[...] = packets.reshape(slots.shape)

    def peer(a, b):
        return lax.rem(z + a, BEAM) * GROUP + lax.rem(y + b, GROUP)

    def source(a, b):
        return lax.rem(z + BEAM - a, BEAM) * GROUP + lax.rem(y + GROUP - b, GROUP)

    home = held.at[x, core]
    stay = pltpu.make_async_copy(slots.at[ex], home.at[ex], local.at[0])
    stay.start()
    for a in ORDER:
        for b in range(GROUP):
            if a or b:
                spot = a * GROUP + b
                move = send(slots.at[peer(a, b)], home.at[ex], d_send.at[spot], d_recv.at[spot], dp, peer(a, b))
                move.start()
                sent.append(move)

    def chunk(which, owner, j):
        zz = lax.rem(z + BEAM - ORDER[j], BEAM)
        return held.at[chip[which], owner, pl.ds(zz * GROUP, GROUP)]

    def to_sibling(which, j):
        part = chunk(which, core, j)
        move = send(part, part, t_send.at[which, j], t_recv.at[which, j], twin, ex)
        move.start()
        sent.append(move)

    def from_sibling(which):
        for j in range(4):
            part = chunk(which, 1 - core, j)
            send(part, part, t_send.at[which, j], t_recv.at[which, j], twin, ex).wait_recv()

    stay.wait()
    for j, a in enumerate(ORDER):
        for b in range(GROUP):
            if a or b:
                spot = a * GROUP + b
                there = home.at[source(a, b)]
                send(there, there, d_send.at[spot], d_recv.at[spot], dp, source(a, b)).wait_recv()
        part = chunk(OWN, core, j)
        for way, side in ((0, RIGHT), (1, LEFT)):
            move = send(part, part, g_send.at[way, j], g_recv.at[way, j], chip[side] * 2 + core, ex)
            move.start()
            sent.append(move)
        to_sibling(OWN, j)

    cells = picked.shape[0] // 2
    tile = min(1024, hidden)
    wide = min(1024, width)
    slim = min(256, width)
    band = block // 4

    def up(which):
        for half, owner in ((0, core), (1, 1 - core)):
            picked[half * cells : (half + 1) * cells, :] = held[chip[which], owner].reshape(cells, width)

        @pl.loop(0, hidden // tile)
        def _(n):
            spot = pl.ds(pl.multiple_of(n * tile, tile), tile)
            part = jnp.dot(picked[...], first_v[:, spot], preferred_element_type=jnp.float32)
            inner[:, spot] = jnp.maximum(part, 0.0).astype(inner.dtype)

    def down(which):
        @pl.loop(0, width // wide)
        def _(n):
            spot = pl.ds(pl.multiple_of(n * wide, wide), wide)
            part = jnp.dot(inner[...], second_v[:, spot], preferred_element_type=jnp.float32)
            total[which, :, spot] = part[:cells]
            to_twin[which, :, spot] = part[cells:].astype(to_twin.dtype)

        move = send(to_twin.at[which], from_twin.at[which], y_send.at[which], y_recv.at[which], twin, ex)
        move.start()
        sent.append(move)

    def forward(which):
        there = from_twin.at[which]
        send(there, there, y_send.at[which], y_recv.at[which], twin, ex).wait_recv()

        @pl.loop(0, width // slim)
        def _(n):
            spot = pl.ds(pl.multiple_of(n * slim, slim), slim)
            both = total[which, :, spot] + from_twin[which, :, spot].astype(jnp.float32)
            to_chip[which - 1, :, spot] = both.astype(to_chip.dtype)

        if which == OPPOSITE:
            for q in (0, 2, 1, 3):
                rows = pl.ds(q * band, band)
                relay(to_chip.at[2, rows], far.at[rows], f_send.at[q], f_recv.at[q], RIGHT if q < 2 else LEFT)
        else:
            for q in (2, 3) if which == RIGHT else (0, 1):
                last_leg(which, q)

    def relay(src, dst, send_sem, recv_sem, side):
        move = send(src, dst, send_sem, recv_sem, chip[side] * 2 + core, ex)
        move.start()
        sent.append(move)

    def last_leg(which, q):
        rows = pl.ds(q * band, band)
        spot = which - 1
        relay(to_chip.at[spot, rows], from_chip.at[spot, rows], x_send.at[spot, q], x_recv.at[spot, q], which)

    def merge(q):
        rows = pl.ds(q * band, band)
        which = RIGHT if q < 2 else LEFT
        there = far.at[rows]
        send(there, there, f_send.at[q], f_recv.at[q], dp, ex).wait_recv()

        @pl.loop(0, width // slim)
        def _(n):
            spot = pl.ds(pl.multiple_of(n * slim, slim), slim)
            both = to_chip[which - 1, rows, spot].astype(jnp.float32) + far[rows, spot].astype(jnp.float32)
            to_chip[which - 1, rows, spot] = both.astype(to_chip.dtype)

        last_leg(which, q)

    def landed(way, j):
        side = LEFT if way == 0 else RIGHT
        part = chunk(side, core, j)
        send(part, part, g_send.at[way, j], g_recv.at[way, j], dp, ex).wait_recv()
        to_sibling(side, j)
        if (j < 2) == (way == 0):
            onward = RIGHT if way == 0 else LEFT
            move = send(part, part, o_send.at[j], o_recv.at[j], chip[onward] * 2 + core, ex)
            move.start()
            sent.append(move)

    paged = []
    for off in (1, 3, 2):
        move = send(
            pages.at[off - 1], arrived.at[off - 1], p_send.at[off - 1], p_recv.at[off - 1],
            dp, lax.rem(z + off, BEAM) * GROUP + y,
        )
        move.start()
        paged.append(move)
    for load in loads[:2]:
        load.wait()
    from_sibling(OWN)
    up(OWN)
    down(OWN)
    for j in range(4):
        landed(0, j)
        landed(1, j)
    from_sibling(LEFT)
    up(LEFT)
    down(LEFT)
    from_sibling(RIGHT)
    up(RIGHT)
    forward(LEFT)
    down(RIGHT)
    for j in range(4):
        part = chunk(OPPOSITE, core, j)
        send(part, part, o_send.at[j], o_recv.at[j], dp, ex).wait_recv()
        to_sibling(OPPOSITE, j)
    from_sibling(OPPOSITE)
    up(OPPOSITE)
    forward(RIGHT)
    down(OPPOSITE)
    forward(OPPOSITE)
    for q in (0, 2, 1, 3):
        merge(q)

    there = from_twin.at[OWN]
    send(there, there, y_send.at[OWN], y_recv.at[OWN], twin, ex).wait_recv()
    cap = block // EXPERTS
    stay = pltpu.make_async_copy(result.at[ex], returned.at[ex], local.at[1])
    for q in (0, 2, 1, 3):
        rows = pl.ds(q * band, band)
        for spot in (0, 1):
            there = from_chip.at[spot, rows]
            send(there, there, x_send.at[spot, q], x_recv.at[spot, q], dp, ex).wait_recv()

        @pl.loop(0, width // slim)
        def _(n):
            spot = pl.ds(pl.multiple_of(n * slim, slim), slim)
            whole = total[OWN, rows, spot] + from_twin[OWN, rows, spot].astype(jnp.float32)
            for side in (0, 1):
                whole = whole + from_chip[side, rows, spot].astype(jnp.float32)
            packets = whole.astype(result.dtype).reshape(GROUP, cap, slim)
            result[q * GROUP : (q + 1) * GROUP, :, spot] = packets

        for target in range(q * GROUP, (q + 1) * GROUP):
            move = send(result.at[target], returned.at[ex], r_send.at[target], r_recv.at[ex], dp, target)
            pl.when(target != ex)(move.start)
            pl.when(target == ex)(stay.start)
    for origin in range(EXPERTS):
        there = returned.at[origin]
        move = send(there, there, r_send.at[origin], r_recv.at[origin], dp, origin)
        pl.when(origin != ex)(move.wait)
    stay.wait()
    back = returned[...].reshape(block, width)
    places = lax.broadcasted_iota(jnp.int32, (row_count, block), 1).astype(jnp.float32)
    final = hidden_v[...]
    for k in range(2):
        taken = (places == info_v[:, 1 + k : 2 + k]).astype(kind)
        final = final + info_v[:, 3 + k : 4 + k] * jnp.dot(taken, back, preferred_element_type=jnp.float32)
    mixed[...] = final.astype(mixed.dtype)
    for move in sent:
        move.wait_send()
    for move in paged:
        move.wait()


def batch_of(heads):
    return math.gcd(heads, 4)


def layer(query, cross, lanes, info, tokens, new_kv, gain, cache, memory, first, second):
    row_count, width = tokens.shape
    hidden = first.shape[-1]
    kind = tokens.dtype
    cap = 4 * row_count // EXPERTS
    block = EXPERTS * cap
    quarter = row_count // BEAM

    def room(*shape, dtype=kind):
        return pltpu.VMEM(shape, dtype)

    paged = (BEAM - 1, PAGE_CAP) + cache.shape[1:]
    scratch = [
        room(*cache.shape), room(*memory.shape), room(row_count, width), room(row_count, 2 * width),
        room(1, width, dtype=jnp.float32), room(row_count, HEAD, dtype=jnp.float32),
        room(BEAM, row_count, width), room(BEAM, *lanes.shape, dtype=jnp.int32), room(BEAM, quarter, width),
        room(BEAM, row_count, width), room(BEAM, row_count, HEAD, dtype=jnp.float32), room(BEAM, quarter, width),
        room(BEAM, row_count, width), room(BEAM, row_count, HEAD, dtype=jnp.float32), room(BEAM, quarter, width),
        room(row_count, width, dtype=jnp.float32), room(*paged), room(EXPERTS, cap, width), room(EXPERTS, cap, width),
        room(CHIPS, 2, EXPERTS, cap, width), room(*first.shape), room(*second.shape),
        room(2 * block, width), room(2 * block, hidden), room(4, block, width, dtype=jnp.float32),
        room(4, block, width), room(4, block, width), room(3, block, width), room(2, block, width),
        room(block, width), room(EXPERTS, cap, width),
    ]
    sems = [
        DMA((10,)), DMA((3,)), DMA((3,)), DMA((3,)), DMA((3,)), DMA((3,)), DMA((4,)), DMA((4,)),
        DMA((3,)), DMA((3,)), DMA((3,)), DMA((3,)), DMA((4,)), DMA((4,)),
        DMA((16,)), DMA((16,)), DMA((16,)), DMA((16,)),
        DMA((2, 4)), DMA((2, 4)), DMA((4,)), DMA((4,)), DMA((4, 4)), DMA((4, 4)),
        DMA((4,)), DMA((4,)), DMA((2, 4)), DMA((2, 4)), DMA((4,)), DMA((4,)), DMA((3,)), DMA((3,)),
    ]
    return pl.pallas_call(
        layer_kernel,
        out_shape=[jax.ShapeDtypeStruct((row_count, width), kind), jax.ShapeDtypeStruct(paged, kind)],
        in_specs=[ANY] * 11,
        out_specs=[pl.BlockSpec(memory_space=pltpu.VMEM), ANY],
        scratch_shapes=scratch + sems,
        compiler_params=pltpu.CompilerParams(
            collective_id=0, has_side_effects=True, vmem_limit_bytes=58 * 2**20
        ),
        name="layer",
    )(query, cross, lanes, info, tokens, new_kv, gain, cache, memory, first, second)


def per_device(
    tokens,
    self_query,
    new_kv,
    kv_cache,
    parents,
    dec_len,
    cross_query,
    memory,
    src_len,
    norm_gain,
    routes,
    gate_weights,
    expert_in,
    expert_out,
):
    row_count, model_width = tokens.shape
    span = kv_cache.shape[1]
    quarter, reach = memory.shape[:2]
    slot_cap = 4 * row_count // EXPERTS
    sub_pos = lax.axis_index("expert") % GROUP
    lengths = lax.dynamic_slice_in_dim(dec_len, sub_pos * row_count, row_count)
    order = jnp.arange(row_count, dtype=jnp.int32)
    earlier = order[:, None] > order[None, :]
    rank = jnp.sum((earlier & (parents[:, None] == parents[None, :])).astype(jnp.int32), 1)
    alike = routes[:, :, None, None] == routes[None, None, :, :]
    slot = jnp.sum((alike & earlier[:, None, :, None]).astype(jnp.int32), (2, 3)) + routes * slot_cap
    long = max(quarter * reach, row_count * span)

    def line(values):
        return jnp.pad(values, (0, long - values.shape[0]))

    lanes = jnp.stack(
        [
            line(jnp.repeat(lengths, span)),
            line(jnp.repeat(src_len, reach)),
            line(slot[:, 0]),
            line(slot[:, 1]),
            line(jnp.repeat(parents, span)),
            line(jnp.repeat(rank, span)),
            jnp.zeros((long,), jnp.int32),
            jnp.zeros((long,), jnp.int32),
        ]
    )
    info = jnp.concatenate([parents[:, None].astype(jnp.float32), slot.astype(jnp.float32), gate_weights], 1)
    info = jnp.pad(info, ((0, 0), (0, HEAD - info.shape[1])))
    mixed, arrived = layer(
        self_query,
        cross_query.reshape(GROUP, quarter, model_width),
        lanes,
        info,
        tokens,
        new_kv,
        norm_gain[None],
        kv_cache,
        memory,
        expert_in[0],
        expert_out[0],
    )
    return (mixed, unpack(parents, kv_cache, arrived))


def solution(mesh):
    placed = (
        P(("dp", "expert"), None),
        P(("dp", "expert"), None),
        P(("dp", "expert"), None),
        P(("dp", "expert"), None, None),
        P(("dp", "expert")),
        P("dp"),
        P(("dp", "expert"), None),
        P(("dp", "expert"), None, None),
        P(("dp", "expert")),
        P(),
        P(("dp", "expert"), None),
        P(("dp", "expert"), None),
        P("expert", None, "dp"),
        P("expert", "dp", None),
    )
    return jax.shard_map(
        per_device,
        mesh=mesh,
        in_specs=placed,
        out_specs=(P(("dp", "expert"), None), P(("dp", "expert"), None, None)),
        check_vma=False,
    )
```

time: 135 us -> 110 us (0.81)
  Pallas kernels: 110 us -> 100 us
  matrix products: 7.85 us -> 0 us
  local copies, waits for them, and re-layouts: 10.8 us -> 4.69 us
  other arithmetic: 5.36 us -> 3.89 us
    dot_general x6 -> x0, matrix products: 7.85 us -> none  [the longest x1 3.11 us: per_device(): jnp.einsum('brhp,rphk->brhk', weights, values, preferred_element_type=jnp...]
    pallas_call x4 -> x1, Pallas kernels: 104 us -> 96.7 us  [layer(): pl.pallas_call(layer_kernel, out_shape=[jax.ShapeDtypeStruct((row_count,...]
    unnamed x33 -> x3, local copies, waits for them, and re-layouts: 5.69 us -> 0.66 us
    reduce_sum x7 -> x2, other arithmetic: 3.8 us -> 1.85 us  [the longest x1 0.94 us: per_device(): jnp.sum((alike & earlier[:, None, :, None]).astype(jnp.int32), (2, 3))]
    pallas_call x1, Pallas kernels: 5.64 us -> 3.77 us  [unpack(): pl.pallas_call(unpack_kernel, out_shape=jax.ShapeDtypeStruct(cache.shape,...]
    broadcast_in_dim x0 -> x4, local copies, waits for them, and re-layouts: none -> 1.59 us  [the longest x1 0.73 us: per_device(): jnp.repeat(parents, span)]
where the time goes in v3:
time: 110 us
  Pallas kernels  100 us (91%)
  local copies, waits for them, and re-layouts  4.69 us (4%)
  other arithmetic  3.89 us (4%)
    pallas_call x1, Pallas kernels, layer(): pl.pallas_call(layer_kernel, out_shape=[jax.ShapeDtypeStruct((row_count,...  96.7 us
    pallas_call x1, Pallas kernels, unpack(): pl.pallas_call(unpack_kernel, out_shape=jax.ShapeDtypeStruct(cache.shape,...  3.77 us

profile of v3, /device:TPU:0, one launch (start us, length us, event | category | flops | bytes accessed | tf_op | source)
XLA Modules:
  0.0 109.8 jit_solution(3927982612476283672)
XLA Ops:
  0.6 0.7 dynamic_slice.3
  1.4 0.9 convert_reduce_fusion.1
  2.3 0.7 convert_bitcast_fusion
  3.0 0.7 broadcast_in_dim.11
  3.7 0.1 stack.25
  3.8 0.9 convert_reduce_fusion
  4.7 0.7 fusion
  5.4 0.7 pad_maximum_fusion
  6.1 0.1 copy.31
  6.2 0.6 pad.26.info
  6.8 0.1 broadcast_in_dim.26
  6.9 0.1 reshape.38
  7.0 0.1 broadcast_in_dim.10
  7.0 0.1 reshape.36
  7.2 0.7 broadcast_in_dim.12
  7.9 0.1 reshape.37
  8.0 0.6 stack.31.lanes
  8.6 96.7 %layer.1 = (bf16[32,2048]{1,0:T(8,128)(2,1)}, bf16[3,16,8,4096]{3,2,1,0:T(8,128)(2,1)}) custom-call(bf16[32,2048]{1,0:T(8,128)(2,1)} %query.1, bf16[4,8,2048]{2,1,0:T(8,128)(2,1)} %bitcast.17, s32[8,512]{1,0:T(8,128)} %stack.31.lanes, f32[32,128]{1,0:T(8,128)} %pad.26.info, bf16[32,2048]{1,0:T(8,128)(2,1)} %tokens.1, bf16[32,4096]{1,0:T(8,128)(2,1)} %new_kv.1, ...), custom_call_target="tpu_custom_call" | custom-call | tf_op jit(solution)/shard_map/layer/pallas_call | solution.py:534
  105.3 0.0 copy-start
  105.3 3.8 %unpack.1 = bf16[32,8,4096]{2,1,0:T(8,128)(2,1)} custom-call(s32[32]{0:T(128)} %parents.1, bf16[32,8,4096]{2,1,0:T(8,128)(2,1)} %cache.3, bf16[3,16,8,4096]{3,2,1,0:T(8,128)(2,1)} %get-tuple-element.5.arrived), custom_call_target="tpu_custom_call" | custom-call | tf_op jit(solution)/shard_map/unpack/pallas_call | solution.py:71
  109.1 0.0 copy-done
  109.1 0.7 copy.33
  (8 shorter events, 0.0 us)
Async XLA Ops:
  105.3 3.8 %copy-start = (bf16[32,2048]{1,0:T(8,128)(2,1)S(1)}, bf16[32,2048]{1,0:T(8,128)(2,1)}, u32[]{:S(2)}) copy-start(bf16[32,2048]{1,0:T(8,128)(2,1)} %get-tuple-element.12) | copy-start | bytes 393220

commit v4 on v3

--- a/solution.py
+++ b/solution.py
@@ -81,12 +81,47 @@
 
 ORDER = (0, 1, 3, 2)
 OWN, LEFT, RIGHT, OPPOSITE = range(4)
+EARLY = 4
+
+
+def eye(n):
+    shape = (n, n)
+    return lax.broadcasted_iota(jnp.int32, shape, 0) == lax.broadcasted_iota(jnp.int32, shape, 1)
+
+
+def upright(row):
+    return jnp.sum(jnp.where(eye(row.shape[1]), row, 0.0), 1, keepdims=True)
+
+
+def flat(column):
+    return jnp.sum(jnp.where(eye(column.shape[0]), column, 0.0), 0, keepdims=True)
+
+
+def spread(column, times):
+    shape = (column.shape[0], column.shape[0] * times)
+    owner = lax.div(lax.broadcasted_iota(jnp.int32, shape, 1), times)
+    return jnp.sum(jnp.where(owner == lax.broadcasted_iota(jnp.int32, shape, 0), column, 0.0), 0, keepdims=True)
+
+
+def rank(column, rows):
+    shape = (column.shape[0], rows[0].shape[1])
+    earlier = lax.broadcasted_iota(jnp.int32, shape, 1) < lax.broadcasted_iota(jnp.int32, shape, 0)
+    alike = functools.reduce(jnp.logical_or, [column == row for row in rows])
+    return jnp.sum(jnp.where(earlier & alike, 1.0, 0.0), 1, keepdims=True)
+
+
+def number(shape, axis):
+    return lax.broadcasted_iota(jnp.int32, shape, axis)
+
+
+def real(values):
+    return values.astype(jnp.float32)
 
 
 def layer_kernel(
-    query, cross, lanes, info, tokens, new_kv, gain, cache, memory, first, second,
+    query, cross, parents, dec_len, src_len, routes, gates, tokens, new_kv, gain, cache, memory, first, second,
     mixed, arrived,
-    cache_v, memory_v, tokens_v, new_kv_v, gain_v, info_v, queries, wishes, crosses,
+    cache_v, memory_v, tokens_v, new_kv_v, gain_v, query_v, wish, packed, queries, wishes, crosses, bias, bias_c,
     outs, stats, owner_out, got, got_stats, cross_out, hidden_v, pages, slots, returned,
     held, first_v, second_v, picked, inner, total, to_twin, from_twin, to_chip, from_chip, far, result,
     l_sem, local, k_send, k_recv, n_send, n_recv, e_send, e_recv, b_send, b_recv, s_send, s_recv, c_send, c_recv,
@@ -104,7 +139,8 @@
     heads = width // HEAD
     span = cache.shape[1]
     quarter, reach = memory.shape[:2]
-    block = EXPERTS * slots.shape[1]
+    cap = slots.shape[1]
+    block = EXPERTS * cap
     scale = 1.0 / math.sqrt(HEAD)
 
     barrier = pltpu.get_barrier_semaphore()
@@ -116,22 +152,35 @@
     for side in (LEFT, RIGHT, OPPOSITE):
         greet(barrier, chip[side] * 2 + core, ex)
     pairs = (
-        (first, first_v), (second, second_v), (cache, cache_v), (memory, memory_v), (tokens, tokens_v),
-        (new_kv, new_kv_v), (gain, gain_v), (info, info_v), (query, queries.at[z]), (lanes, wishes.at[z]),
+        (query, query_v), (new_kv, new_kv_v), (cache, cache_v), (memory, memory_v),
+        (tokens, tokens_v), (gain, gain_v), (first, first_v), (second, second_v),
     )
     loads = [pltpu.make_async_copy(a, b, l_sem.at[i]) for i, (a, b) in enumerate(pairs)]
-    for i in (9, 8, 2, 5, 3, 4, 6, 7, 0, 1):
-        loads[i].start()
+    for load in loads:
+        load.start()
     own_cross = pltpu.make_async_copy(cross.at[y], crosses.at[z], local.at[2])
     pl.when(z == y)(own_cross.start)
+
+    parent_row = real(parents[...])
+    parent = upright(parent_row)
+    parent_rank = rank(parent, [parent_row])
+    rank_row = flat(parent_rank)
+    ticket = number((BEAM * PAGE_CAP, row_count), 0)
+    chosen = (real(lax.div(ticket, PAGE_CAP)) == parent_row) & (real(lax.rem(ticket, PAGE_CAP)) == rank_row)
+    chosen = real(chosen).astype(kind)
+    wish[0:1, :row_count] = parents[...]
+    loads[0].wait()
+    lines = jnp.dot(chosen, query_v[...], preferred_element_type=jnp.float32).astype(kind)
+    packed[...] = lines.reshape(packed.shape)
     pl.semaphore_wait(barrier, EXPERTS - 1 + 4)
 
     sent = []
     asks = []
     for off in (1, 3, 2):
-        target = lax.rem(z + off, BEAM) * GROUP + y
-        asks.append(send(lanes, wishes.at[z], n_send.at[off - 1], n_recv.at[off - 1], dp, target))
-        asks.append(send(query, queries.at[z], k_send.at[off - 1], k_recv.at[off - 1], dp, target))
+        other = lax.rem(z + off, BEAM)
+        target = other * GROUP + y
+        asks.append(send(wish, wishes.at[z], n_send.at[off - 1], n_recv.at[off - 1], dp, target))
+        asks.append(send(packed.at[other], queries.at[z], k_send.at[off - 1], k_recv.at[off - 1], dp, target))
     for move in asks:
         move.start()
     crossing = [
@@ -139,45 +188,88 @@
     ]
     for p in range(GROUP):
         pl.when(y * GROUP + p != ex)(crossing[p].start)
-
-    for i in (5, 8, 9):
-        loads[i].wait()
-    lane = lax.broadcasted_iota(jnp.int32, (row_count, HEAD), 1)
+    queries[z] = packed[z]
+    wishes[z] = wish[...]
+
+    loads[1].wait()
+    lane = number((row_count, HEAD), 1)
     own = jnp.zeros((row_count, HEAD), jnp.float32)
     for h in range(heads):
         spot = slice(h * HEAD, (h + 1) * HEAD)
-        both = queries[z, :, spot].astype(jnp.float32) * new_kv_v[:, spot].astype(jnp.float32)
+        both = real(query_v[:, spot]) * real(new_kv_v[:, spot])
         own = own + jnp.where(lane == h, jnp.sum(both, -1, keepdims=True) * scale, 0.0)
-
-    asked = BEAM * row_count
-    shape = (asked, row_count * span)
-    lane_row = lax.broadcasted_iota(jnp.int32, shape, 1)
-    same = lax.rem(lax.broadcasted_iota(jnp.int32, shape, 0), row_count) == lax.div(lane_row, span)
+    named_rows = [real(routes[k : k + 1, :]) for k in range(2)]
+    named = [upright(row) for row in named_rows]
+    slot = [column * float(cap) + rank(column, named_rows) for column in named]
+    slot_rows = [flat(column) for column in slot]
+
+    at = number((row_count, dec_len.shape[1]), 1) - y * row_count == number((row_count, dec_len.shape[1]), 0)
+    lengths = jnp.sum(jnp.where(at, real(dec_len[...]), 0.0), 1, keepdims=True)
+    keys = row_count * span
+    in_reach = real(lax.rem(number((1, keys), 1), span)) < spread(lengths, span)
+    keys_c = quarter * reach
+    in_reach_c = real(lax.rem(number((1, keys_c), 1), reach)) < spread(upright(real(src_len[...])), reach)
+    asked_c = BEAM * quarter
+    same_c = lax.rem(number((asked_c, keys_c), 0), quarter) == lax.div(number((asked_c, keys_c), 1), reach)
+    for half in range(2):
+        bias_c[half * asked_c : (half + 1) * asked_c, :] = jnp.where(same_c & in_reach_c, 0.0, -1e30)
+
     loads[2].wait()
     for move in asks:
         move.wait()
-    valid = same & (lax.rem(lane_row, span) < wishes[z, 0:1, : shape[1]])
-    stat_lane = lax.broadcasted_iota(jnp.int32, (asked, HEAD), 1)
+    asked = BEAM * PAGE_CAP
+    ticket = real(number((PAGE_CAP, keys), 0))
+    codes = []
+    for beam in range(BEAM):
+        wanted_row = real(wishes[beam, 0:1, :row_count])
+        wanted = upright(wanted_row)
+        code = spread(jnp.where(wanted == real(z), rank(wanted, [wanted_row]), -1.0), span)
+        codes.append(code)
+        part = jnp.where((ticket == code) & in_reach, 0.0, -1e30)
+        for half in range(2):
+            first_row = half * asked + beam * PAGE_CAP
+            bias[first_row : first_row + PAGE_CAP, :] = part
     stats[...] = jnp.zeros_like(stats)
-
-    @pl.loop(0, heads // batch_of(heads))
+    pair = 2 * HEAD
+    batch = math.gcd(heads // 2, 2)
+
+    def attend(asker, keeper, extra, base):
+        blank = jnp.zeros((asker.shape[0], HEAD), kind)
+        both = jnp.concatenate(
+            [
+                jnp.concatenate([asker[:, :HEAD], blank], 1),
+                jnp.concatenate([blank, asker[:, HEAD:]], 1),
+            ],
+            0,
+        )
+        keys_of = keeper(base)
+        scores = lax.dot_general(both, keys_of, (((1,), (1,)), ((), ())), preferred_element_type=jnp.float32)
+        scores = scores * scale + extra[...]
+        peak = jnp.max(scores, -1, keepdims=True)
+        terms = jnp.exp(scores - peak)
+        mass = jnp.sum(terms, -1, keepdims=True)
+        part = jnp.dot((terms / mass).astype(kind), keeper(width + base), preferred_element_type=jnp.float32)
+        return part.astype(kind), peak + jnp.log(mass)
+
+    stat_lane = number((asked, HEAD), 1)
+
+    @pl.loop(0, heads // 2 // batch)
     def _(n):
-        for m in range(batch_of(heads)):
-            h = n * batch_of(heads) + m
-            spot = pl.ds(pl.multiple_of(h * HEAD, HEAD), HEAD)
-            spot_v = pl.ds(pl.multiple_of(width + h * HEAD, HEAD), HEAD)
-            q_h = queries[:, :, spot].reshape(asked, HEAD)
-            k_h = cache_v[:, :, spot].reshape(row_count * span, HEAD)
-            v_h = cache_v[:, :, spot_v].reshape(row_count * span, HEAD)
-            scores = lax.dot_general(q_h, k_h, (((1,), (1,)), ((), ())), preferred_element_type=jnp.float32)
-            scores = jnp.where(valid, scores * scale, -1e30)
-            peak = jnp.max(scores, -1, keepdims=True)
-            terms = jnp.exp(scores - peak)
-            mass = jnp.sum(terms, -1, keepdims=True)
-            part = jnp.dot((terms / mass).astype(kind), v_h, preferred_element_type=jnp.float32)
-            outs[:, :, spot] = part.astype(kind).reshape(BEAM, row_count, HEAD)
-            level = jnp.where(stat_lane == h, peak + jnp.log(mass), 0.0)
-            stats[...] += level.reshape(BEAM, row_count, HEAD)
+        for m in range(batch):
+            base = (n * batch + m) * pair
+            spot = pl.ds(pl.multiple_of(base, pair), pair)
+
+            def keeper(start):
+                return cache_v[:, :, pl.ds(pl.multiple_of(start, pair), pair)].reshape(keys, pair)
+
+            part, level = attend(queries[:, :, spot].reshape(asked, pair), keeper, bias, base)
+            levels = jnp.zeros((asked, HEAD), jnp.float32)
+            for half in range(2):
+                rows = slice(half * asked, (half + 1) * asked)
+                piece = part[rows, half * HEAD : (half + 1) * HEAD].reshape(BEAM, PAGE_CAP, HEAD)
+                outs[:, :, pl.ds(pl.multiple_of(base + half * HEAD, HEAD), HEAD)] = piece
+                levels = jnp.where(stat_lane == 2 * (n * batch + m) + half, level[rows], levels)
+            stats[...] += levels.reshape(BEAM, PAGE_CAP, HEAD)
 
     answers = []
     for off in (1, 3, 2):
@@ -187,12 +279,8 @@
         answers.append(send(outs.at[other], got.at[z], s_send.at[off - 1], s_recv.at[off - 1], dp, target))
     for move in answers:
         move.start()
-    stays = [
-        pltpu.make_async_copy(outs.at[z], got.at[z], local.at[0]),
-        pltpu.make_async_copy(stats.at[z], got_stats.at[z], local.at[1]),
-    ]
-    for stay in stays:
-        stay.start()
+    got[z] = outs[z]
+    got_stats[z] = stats[z]
 
     for p in range(GROUP):
         pl.when(y * GROUP + p != ex)(crossing[p].wait_send)
@@ -201,28 +289,21 @@
         pl.when(beam * GROUP + z != ex)(coming.wait_recv)
     pl.when(z == y)(own_cross.wait)
     loads[3].wait()
-    asked_c = BEAM * quarter
-    shape_c = (asked_c, quarter * reach)
-    lane_c = lax.broadcasted_iota(jnp.int32, shape_c, 1)
-    same_c = lax.rem(lax.broadcasted_iota(jnp.int32, shape_c, 0), quarter) == lax.div(lane_c, reach)
-    valid_c = same_c & (lax.rem(lane_c, reach) < wishes[z, 1:2, : shape_c[1]])
-
-    @pl.loop(0, heads // batch_of(heads))
+
+    @pl.loop(0, heads // 2 // batch)
     def _(n):
-        for m in range(batch_of(heads)):
-            h = n * batch_of(heads) + m
-            spot = pl.ds(pl.multiple_of(h * HEAD, HEAD), HEAD)
-            spot_v = pl.ds(pl.multiple_of(width + h * HEAD, HEAD), HEAD)
-            q_h = crosses[:, :, spot].reshape(asked_c, HEAD)
-            k_h = memory_v[:, :, spot].reshape(quarter * reach, HEAD)
-            v_h = memory_v[:, :, spot_v].reshape(quarter * reach, HEAD)
-            scores = lax.dot_general(q_h, k_h, (((1,), (1,)), ((), ())), preferred_element_type=jnp.float32)
-            scores = jnp.where(valid_c, scores * scale, -1e30)
-            peak = jnp.max(scores, -1, keepdims=True)
-            terms = jnp.exp(scores - peak)
-            mass = jnp.sum(terms, -1, keepdims=True)
-            part = jnp.dot((terms / mass).astype(kind), v_h, preferred_element_type=jnp.float32)
-            owner_out[:, :, spot] = part.astype(kind).reshape(BEAM, quarter, HEAD)
+        for m in range(batch):
+            base = (n * batch + m) * pair
+            spot = pl.ds(pl.multiple_of(base, pair), pair)
+
+            def keeper(start):
+                return memory_v[:, :, pl.ds(pl.multiple_of(start, pair), pair)].reshape(keys_c, pair)
+
+            part, _ = attend(crosses[:, :, spot].reshape(asked_c, pair), keeper, bias_c, base)
+            for half in range(2):
+                piece = part[half * asked_c : (half + 1) * asked_c, half * HEAD : (half + 1) * HEAD]
+                place_at = pl.ds(pl.multiple_of(base + half * HEAD, HEAD), HEAD)
+                owner_out[:, :, place_at] = piece.reshape(BEAM, quarter, HEAD)
 
     own_back = pltpu.make_async_copy(owner_out.at[z], cross_out.at[y], local.at[2])
     crossing = [
@@ -233,29 +314,40 @@
         pl.when(beam * GROUP + z != ex)(crossing[beam].start)
     pl.when(z == y)(own_back.start)
 
-    page_shape = (PAGE_CAP * span, row_count * span)
-    page_row = lax.broadcasted_iota(jnp.int32, page_shape, 0)
-    page_lane = lax.broadcasted_iota(jnp.int32, page_shape, 1)
-    page_slot = lax.div(page_row, span)
+    paged = []
+
+    def turn(off, start, stop, which):
+        rows = pl.ds(start, stop - start)
+        move = send(
+            pages.at[off - 1, rows], arrived.at[off - 1, rows], p_send.at[off - 1, which], p_recv.at[off - 1, which],
+            dp, lax.rem(z + off, BEAM) * GROUP + y,
+        )
+        move.start()
+        paged.append(move)
+
+    page_shape = (PAGE_CAP * span, keys)
+    page_row, page_lane = number(page_shape, 0), number(page_shape, 1)
+    page_slot = real(lax.div(page_row, span))
     same_place = lax.rem(page_row, span) == lax.rem(page_lane, span)
     strip = min(1024, 2 * width)
     for off in (1, 3, 2):
         asker = lax.rem(z + off, BEAM)
-        wanted = wishes[asker, 4:5, : page_shape[1]] == z
-        pick = same_place & wanted & (page_slot == wishes[asker, 5:6, : page_shape[1]])
-        pick = pick.astype(jnp.float32).astype(kind)
+        code = jnp.zeros_like(codes[0])
+        for beam in range(BEAM):
+            code = code + jnp.where(real(asker) == float(beam), codes[beam], 0.0)
+        pick = real(same_place & (page_slot == code)).astype(kind)
 
         @pl.loop(0, 2 * width // strip)
         def _(n):
             spot = pl.ds(pl.multiple_of(n * strip, strip), strip)
-            lines = cache_v[:, :, spot].reshape(row_count * span, strip)
-            part = jnp.dot(pick, lines, preferred_element_type=jnp.float32).astype(kind)
-            pages[off - 1, :, :, spot] = part.reshape(PAGE_CAP, span, strip)
-
-    for load in loads[4:5] + loads[6:8]:
+            part = jnp.dot(pick, cache_v[:, :, spot].reshape(keys, strip), preferred_element_type=jnp.float32)
+            pages[off - 1, :, :, spot] = part.astype(kind).reshape(PAGE_CAP, span, strip)
+
+        if off != 2 and EARLY:
+            turn(off, 0, EARLY, 0)
+
+    for load in loads[4:6]:
         load.wait()
-    for stay in stays:
-        stay.wait()
     for move in answers:
         move.wait()
     for beam in range(BEAM):
@@ -265,10 +357,16 @@
         pl.when(y * GROUP + p != ex)(coming.wait_recv)
     pl.when(z == y)(own_back.wait)
 
-    parent = info_v[:, 0:1]
-    level = jnp.zeros((row_count, HEAD), jnp.float32)
-    for beam in range(BEAM):
-        level = level + jnp.where(parent == float(beam), got_stats[beam], 0.0)
+    ticket = number((row_count, asked), 1)
+    chosen = (parent == real(lax.div(ticket, PAGE_CAP))) & (parent_rank == real(lax.rem(ticket, PAGE_CAP)))
+    chosen = real(chosen)
+    level = jnp.dot(
+        chosen,
+        got_stats[...].reshape(asked, HEAD),
+        precision=lax.Precision.HIGHEST,
+        preferred_element_type=jnp.float32,
+    )
+    cached = jnp.dot(chosen.astype(kind), got[...].reshape(asked, width), preferred_element_type=jnp.float32)
     top = jnp.maximum(level, own)
     cache_part = jnp.exp(level - top)
     own_part = jnp.exp(own - top)
@@ -276,20 +374,16 @@
     own_share = own_part / (cache_part + own_part)
     for h in range(heads):
         spot = slice(h * HEAD, (h + 1) * HEAD)
-        cached = jnp.zeros((row_count, HEAD), jnp.float32)
-        for beam in range(BEAM):
-            cached = cached + jnp.where(parent == float(beam), got[beam, :, spot].astype(jnp.float32), 0.0)
-        own_value = new_kv_v[:, width + h * HEAD : width + (h + 1) * HEAD].astype(jnp.float32)
-        mine = cache_share[:, h : h + 1] * cached + own_share[:, h : h + 1] * own_value
-        crossed = cross_out[:, :, spot].reshape(row_count, HEAD).astype(jnp.float32)
-        hidden_v[:, spot] = tokens_v[:, spot].astype(jnp.float32) + mine + crossed
+        own_value = real(new_kv_v[:, width + h * HEAD : width + (h + 1) * HEAD])
+        mine = cache_share[:, h : h + 1] * cached[:, spot] + own_share[:, h : h + 1] * own_value
+        crossed = real(cross_out[:, :, spot].reshape(row_count, HEAD))
+        hidden_v[:, spot] = real(tokens_v[:, spot]) + mine + crossed
     whole = hidden_v[...]
     centered = whole - jnp.mean(whole, -1, keepdims=True)
     variance = jnp.mean(centered * centered, -1, keepdims=True)
     moe_in = (centered * lax.rsqrt(variance + 1e-05) * gain_v[...]).astype(kind)
-    slot_row = lax.broadcasted_iota(jnp.int32, (block, row_count), 0)
-    table = (slot_row == wishes[z, 2:3, :row_count]) | (slot_row == wishes[z, 3:4, :row_count])
-    table = table.astype(jnp.float32).astype(kind)
+    slot_row = real(number((block, row_count), 0))
+    table = real((slot_row == slot_rows[0]) | (slot_row == slot_rows[1])).astype(kind)
     packets = jnp.dot(table, moe_in, preferred_element_type=jnp.float32).astype(kind)
     slots[...] = packets.reshape(slots.shape)
 
@@ -420,15 +514,10 @@
             move.start()
             sent.append(move)
 
-    paged = []
     for off in (1, 3, 2):
-        move = send(
-            pages.at[off - 1], arrived.at[off - 1], p_send.at[off - 1], p_recv.at[off - 1],
-            dp, lax.rem(z + off, BEAM) * GROUP + y,
-        )
-        move.start()
-        paged.append(move)
-    for load in loads[:2]:
+        begin = EARLY if off != 2 else 0
+        turn(off, begin, PAGE_CAP, 1)
+    for load in loads[6:8]:
         load.wait()
     from_sibling(OWN)
     up(OWN)
@@ -457,7 +546,6 @@
 
     there = from_twin.at[OWN]
     send(there, there, y_send.at[OWN], y_recv.at[OWN], twin, ex).wait_recv()
-    cap = block // EXPERTS
     stay = pltpu.make_async_copy(result.at[ex], returned.at[ex], local.at[1])
     for q in (0, 2, 1, 3):
         rows = pl.ds(q * band, band)
@@ -484,11 +572,11 @@
         pl.when(origin != ex)(move.wait)
     stay.wait()
     back = returned[...].reshape(block, width)
-    places = lax.broadcasted_iota(jnp.int32, (row_count, block), 1).astype(jnp.float32)
+    places = real(number((row_count, block), 1))
     final = hidden_v[...]
     for k in range(2):
-        taken = (places == info_v[:, 1 + k : 2 + k]).astype(kind)
-        final = final + info_v[:, 3 + k : 4 + k] * jnp.dot(taken, back, preferred_element_type=jnp.float32)
+        taken = real(places == slot[k]).astype(kind)
+        final = final + upright(gates[k : k + 1, :]) * jnp.dot(taken, back, preferred_element_type=jnp.float32)
     mixed[...] = final.astype(mixed.dtype)
     for move in sent:
         move.wait_send()
@@ -496,11 +584,8 @@
         move.wait()
 
 
-def batch_of(heads):
-    return math.gcd(heads, 4)
-
-
-def layer(query, cross, lanes, info, tokens, new_kv, gain, cache, memory, first, second):
+def layer(*operands):
+    tokens, _, _, cache, memory, first, second = operands[7:]
     row_count, width = tokens.shape
     hidden = first.shape[-1]
     kind = tokens.dtype
@@ -514,10 +599,12 @@
     paged = (BEAM - 1, PAGE_CAP) + cache.shape[1:]
     scratch = [
         room(*cache.shape), room(*memory.shape), room(row_count, width), room(row_count, 2 * width),
-        room(1, width, dtype=jnp.float32), room(row_count, HEAD, dtype=jnp.float32),
-        room(BEAM, row_count, width), room(BEAM, *lanes.shape, dtype=jnp.int32), room(BEAM, quarter, width),
-        room(BEAM, row_count, width), room(BEAM, row_count, HEAD, dtype=jnp.float32), room(BEAM, quarter, width),
-        room(BEAM, row_count, width), room(BEAM, row_count, HEAD, dtype=jnp.float32), room(BEAM, quarter, width),
+        room(1, width, dtype=jnp.float32), room(row_count, width), room(8, HEAD, dtype=jnp.int32),
+        room(BEAM, PAGE_CAP, width), room(BEAM, PAGE_CAP, width), room(BEAM, 8, HEAD, dtype=jnp.int32),
+        room(BEAM, quarter, width), room(2 * BEAM * PAGE_CAP, row_count * cache.shape[1], dtype=jnp.float32),
+        room(2 * BEAM * quarter, quarter * memory.shape[1], dtype=jnp.float32),
+        room(BEAM, PAGE_CAP, width), room(BEAM, PAGE_CAP, HEAD, dtype=jnp.float32), room(BEAM, quarter, width),
+        room(BEAM, PAGE_CAP, width), room(BEAM, PAGE_CAP, HEAD, dtype=jnp.float32), room(BEAM, quarter, width),
         room(row_count, width, dtype=jnp.float32), room(*paged), room(EXPERTS, cap, width), room(EXPERTS, cap, width),
         room(CHIPS, 2, EXPERTS, cap, width), room(*first.shape), room(*second.shape),
         room(2 * block, width), room(2 * block, hidden), room(4, block, width, dtype=jnp.float32),
@@ -525,23 +612,23 @@
         room(block, width), room(EXPERTS, cap, width),
     ]
     sems = [
-        DMA((10,)), DMA((3,)), DMA((3,)), DMA((3,)), DMA((3,)), DMA((3,)), DMA((4,)), DMA((4,)),
+        DMA((8,)), DMA((3,)), DMA((3,)), DMA((3,)), DMA((3,)), DMA((3,)), DMA((4,)), DMA((4,)),
         DMA((3,)), DMA((3,)), DMA((3,)), DMA((3,)), DMA((4,)), DMA((4,)),
         DMA((16,)), DMA((16,)), DMA((16,)), DMA((16,)),
         DMA((2, 4)), DMA((2, 4)), DMA((4,)), DMA((4,)), DMA((4, 4)), DMA((4, 4)),
-        DMA((4,)), DMA((4,)), DMA((2, 4)), DMA((2, 4)), DMA((4,)), DMA((4,)), DMA((3,)), DMA((3,)),
+        DMA((4,)), DMA((4,)), DMA((2, 4)), DMA((2, 4)), DMA((4,)), DMA((4,)), DMA((3, 2)), DMA((3, 2)),
     ]
     return pl.pallas_call(
         layer_kernel,
         out_shape=[jax.ShapeDtypeStruct((row_count, width), kind), jax.ShapeDtypeStruct(paged, kind)],
-        in_specs=[ANY] * 11,
+        in_specs=[ANY] * 2 + [pl.BlockSpec(memory_space=pltpu.VMEM)] * 5 + [ANY] * 7,
         out_specs=[pl.BlockSpec(memory_space=pltpu.VMEM), ANY],
         scratch_shapes=scratch + sems,
         compiler_params=pltpu.CompilerParams(
             collective_id=0, has_side_effects=True, vmem_limit_bytes=58 * 2**20
         ),
         name="layer",
-    )(query, cross, lanes, info, tokens, new_kv, gain, cache, memory, first, second)
+    )(*operands)
 
 
 def per_device(
@@ -561,40 +648,14 @@
     expert_out,
 ):
     row_count, model_width = tokens.shape
-    span = kv_cache.shape[1]
-    quarter, reach = memory.shape[:2]
-    slot_cap = 4 * row_count // EXPERTS
-    sub_pos = lax.axis_index("expert") % GROUP
-    lengths = lax.dynamic_slice_in_dim(dec_len, sub_pos * row_count, row_count)
-    order = jnp.arange(row_count, dtype=jnp.int32)
-    earlier = order[:, None] > order[None, :]
-    rank = jnp.sum((earlier & (parents[:, None] == parents[None, :])).astype(jnp.int32), 1)
-    alike = routes[:, :, None, None] == routes[None, None, :, :]
-    slot = jnp.sum((alike & earlier[:, None, :, None]).astype(jnp.int32), (2, 3)) + routes * slot_cap
-    long = max(quarter * reach, row_count * span)
-
-    def line(values):
-        return jnp.pad(values, (0, long - values.shape[0]))
-
-    lanes = jnp.stack(
-        [
-            line(jnp.repeat(lengths, span)),
-            line(jnp.repeat(src_len, reach)),
-            line(slot[:, 0]),
-            line(slot[:, 1]),
-            line(jnp.repeat(parents, span)),
-            line(jnp.repeat(rank, span)),
-            jnp.zeros((long,), jnp.int32),
-            jnp.zeros((long,), jnp.int32),
-        ]
-    )
-    info = jnp.concatenate([parents[:, None].astype(jnp.float32), slot.astype(jnp.float32), gate_weights], 1)
-    info = jnp.pad(info, ((0, 0), (0, HEAD - info.shape[1])))
     mixed, arrived = layer(
         self_query,
-        cross_query.reshape(GROUP, quarter, model_width),
-        lanes,
-        info,
+        cross_query.reshape(GROUP, row_count // BEAM, model_width),
+        parents[None],
+        dec_len[None],
+        src_len[None],
+        routes.T,
+        gate_weights.T,
         tokens,
         new_kv,
         norm_gain[None],

time: 110 us -> 95.4 us (0.87); the launches traced: 110 us -> 93.6 us
  Pallas kernels: 100 us -> 92.3 us
  local copies, waits for them, and re-layouts: 4.69 us -> 0.66 us
  other arithmetic: 3.89 us -> 0 us
    pallas_call x1, Pallas kernels: 96.7 us -> 88.5 us  [layer(): pl.pallas_call(layer_kernel, out_shape=[jax.ShapeDtypeStruct((row_count,...]
    reduce_sum x2 -> x0, other arithmetic: 1.85 us -> none  [the longest x1 0.94 us: per_device(): jnp.sum((alike & earlier[:, None, :, None]).astype(jnp.int32), (2, 3))]
    broadcast_in_dim x4 -> x0, local copies, waits for them, and re-layouts: 1.59 us -> none  [the longest x1 0.73 us: per_device(): jnp.repeat(parents, span)]
    convert_element_type x2 -> x0, other arithmetic: 1.35 us -> none  [the longest x1 0.69 us: per_device(): slot.astype(jnp.float32)]
where the time goes in v4:
time: 95.4 us; the launch traced here: 93.6 us
  Pallas kernels  92.3 us (97%)
    pallas_call x1, Pallas kernels, layer(): pl.pallas_call(layer_kernel, out_shape=[jax.ShapeDtypeStruct((row_count,...  88.5 us
    pallas_call x1, Pallas kernels, unpack(): pl.pallas_call(unpack_kernel, out_shape=jax.ShapeDtypeStruct(cache.shape,...  3.77 us

profile of v4, /device:TPU:0, one launch (start us, length us, event | category | flops | bytes accessed | tf_op | source)
XLA Modules:
  0.0 93.6 jit_solution(8411548866030215299)
XLA Ops:
  0.6 88.5 %layer.1 = (bf16[32,2048]{1,0:T(8,128)(2,1)}, bf16[3,16,8,4096]{3,2,1,0:T(8,128)(2,1)}) custom-call(bf16[32,2048]{1,0:T(8,128)(2,1)} %query.1, bf16[4,8,2048]{2,1,0:T(8,128)(2,1)} %bitcast.11, s32[1,32]{1,0:T(1,128)} %bitcast.13, s32[1,128]{1,0:T(1,128)} %bitcast.16, s32[1,8]{1,0:T(1,128)} %bitcast.17, s32[2,32]{1,0:T(2,128)} %bitcast.14, f32[2,32]{1,0:T(2,128)} %bitcast.15, ...), custom_call_target="tpu_custom_call" | custom-call | tf_op jit(solution)/shard_map/layer/pallas_call | solution.py:621
  89.1 0.0 copy-start
  89.1 3.8 %unpack.1 = bf16[32,8,4096]{2,1,0:T(8,128)(2,1)} custom-call(s32[32]{0:T(128)} %parents.1, bf16[32,8,4096]{2,1,0:T(8,128)(2,1)} %cache.3, bf16[3,16,8,4096]{3,2,1,0:T(8,128)(2,1)} %get-tuple-element.5.arrived), custom_call_target="tpu_custom_call" | custom-call | tf_op jit(solution)/shard_map/unpack/pallas_call | solution.py:71
  92.9 0.0 copy-done
  92.9 0.7 copy.17
Async XLA Ops:
  89.1 3.8 %copy-start = (bf16[32,2048]{1,0:T(8,128)(2,1)S(1)}, bf16[32,2048]{1,0:T(8,128)(2,1)}, u32[]{:S(2)}) copy-start(bf16[32,2048]{1,0:T(8,128)(2,1)} %get-tuple-element.8) | copy-start | bytes 393220

commit v5 on v4

--- a/solution.py
+++ b/solution.py
@@ -82,6 +82,7 @@
 ORDER = (0, 1, 3, 2)
 OWN, LEFT, RIGHT, OPPOSITE = range(4)
 EARLY = 4
+MID = 2
 
 
 def eye(n):
@@ -156,8 +157,8 @@
         (tokens, tokens_v), (gain, gain_v), (first, first_v), (second, second_v),
     )
     loads = [pltpu.make_async_copy(a, b, l_sem.at[i]) for i, (a, b) in enumerate(pairs)]
-    for load in loads:
-        load.start()
+    for i in (0, 3, 1, 2, 4, 5, 6, 7):
+        loads[i].start()
     own_cross = pltpu.make_async_copy(cross.at[y], crosses.at[z], local.at[2])
     pl.when(z == y)(own_cross.start)
 
@@ -175,6 +176,11 @@
     pl.semaphore_wait(barrier, EXPERTS - 1 + 4)
 
     sent = []
+    crossing = [
+        send(cross.at[p], crosses.at[z], e_send.at[p], e_recv.at[z], dp, y * GROUP + p) for p in range(GROUP)
+    ]
+    for p in range(GROUP):
+        pl.when(y * GROUP + p != ex)(crossing[p].start)
     asks = []
     for off in (1, 3, 2):
         other = lax.rem(z + off, BEAM)
@@ -183,11 +189,6 @@
         asks.append(send(packed.at[other], queries.at[z], k_send.at[off - 1], k_recv.at[off - 1], dp, target))
     for move in asks:
         move.start()
-    crossing = [
-        send(cross.at[p], crosses.at[z], e_send.at[p], e_recv.at[z], dp, y * GROUP + p) for p in range(GROUP)
-    ]
-    for p in range(GROUP):
-        pl.when(y * GROUP + p != ex)(crossing[p].start)
     queries[z] = packed[z]
     wishes[z] = wish[...]
 
@@ -214,24 +215,8 @@
     for half in range(2):
         bias_c[half * asked_c : (half + 1) * asked_c, :] = jnp.where(same_c & in_reach_c, 0.0, -1e30)
 
-    loads[2].wait()
-    for move in asks:
-        move.wait()
-    asked = BEAM * PAGE_CAP
-    ticket = real(number((PAGE_CAP, keys), 0))
-    codes = []
-    for beam in range(BEAM):
-        wanted_row = real(wishes[beam, 0:1, :row_count])
-        wanted = upright(wanted_row)
-        code = spread(jnp.where(wanted == real(z), rank(wanted, [wanted_row]), -1.0), span)
-        codes.append(code)
-        part = jnp.where((ticket == code) & in_reach, 0.0, -1e30)
-        for half in range(2):
-            first_row = half * asked + beam * PAGE_CAP
-            bias[first_row : first_row + PAGE_CAP, :] = part
-    stats[...] = jnp.zeros_like(stats)
     pair = 2 * HEAD
-    batch = math.gcd(heads // 2, 2)
+    batch = math.gcd(heads // 2, 8)
 
     def attend(asker, keeper, extra, base):
         blank = jnp.zeros((asker.shape[0], HEAD), kind)
@@ -251,6 +236,54 @@
         part = jnp.dot((terms / mass).astype(kind), keeper(width + base), preferred_element_type=jnp.float32)
         return part.astype(kind), peak + jnp.log(mass)
 
+    for p in range(GROUP):
+        pl.when(y * GROUP + p != ex)(crossing[p].wait_send)
+    for beam in range(BEAM):
+        coming = send(cross.at[0], crosses.at[beam], e_send.at[0], e_recv.at[beam], dp, beam * GROUP + z)
+        pl.when(beam * GROUP + z != ex)(coming.wait_recv)
+    pl.when(z == y)(own_cross.wait)
+    loads[3].wait()
+
+    @pl.loop(0, heads // 2 // batch)
+    def _(n):
+        for m in range(batch):
+            base = (n * batch + m) * pair
+            spot = pl.ds(pl.multiple_of(base, pair), pair)
+
+            def keeper(start):
+                return memory_v[:, :, pl.ds(pl.multiple_of(start, pair), pair)].reshape(keys_c, pair)
+
+            part, _ = attend(crosses[:, :, spot].reshape(asked_c, pair), keeper, bias_c, base)
+            for half in range(2):
+                piece = part[half * asked_c : (half + 1) * asked_c, half * HEAD : (half + 1) * HEAD]
+                place_at = pl.ds(pl.multiple_of(base + half * HEAD, HEAD), HEAD)
+                owner_out[:, :, place_at] = piece.reshape(BEAM, quarter, HEAD)
+
+    own_back = pltpu.make_async_copy(owner_out.at[z], cross_out.at[y], local.at[2])
+    crossing = [
+        send(owner_out.at[beam], cross_out.at[y], c_send.at[beam], c_recv.at[y], dp, beam * GROUP + z)
+        for beam in range(BEAM)
+    ]
+    for beam in range(BEAM):
+        pl.when(beam * GROUP + z != ex)(crossing[beam].start)
+    pl.when(z == y)(own_back.start)
+
+    loads[2].wait()
+    for move in asks:
+        move.wait()
+    asked = BEAM * PAGE_CAP
+    ticket = real(number((PAGE_CAP, keys), 0))
+    codes = []
+    for beam in range(BEAM):
+        wanted_row = real(wishes[beam, 0:1, :row_count])
+        wanted = upright(wanted_row)
+        code = spread(jnp.where(wanted == real(z), rank(wanted, [wanted_row]), -1.0), span)
+        codes.append(code)
+        part = jnp.where((ticket == code) & in_reach, 0.0, -1e30)
+        for half in range(2):
+            first_row = half * asked + beam * PAGE_CAP
+            bias[first_row : first_row + PAGE_CAP, :] = part
+    stats[...] = jnp.zeros_like(stats)
     stat_lane = number((asked, HEAD), 1)
 
     @pl.loop(0, heads // 2 // batch)
@@ -281,38 +314,6 @@
         move.start()
     got[z] = outs[z]
     got_stats[z] = stats[z]
-
-    for p in range(GROUP):
-        pl.when(y * GROUP + p != ex)(crossing[p].wait_send)
-    for beam in range(BEAM):
-        coming = send(cross.at[0], crosses.at[beam], e_send.at[0], e_recv.at[beam], dp, beam * GROUP + z)
-        pl.when(beam * GROUP + z != ex)(coming.wait_recv)
-    pl.when(z == y)(own_cross.wait)
-    loads[3].wait()
-
-    @pl.loop(0, heads // 2 // batch)
-    def _(n):
-        for m in range(batch):
-            base = (n * batch + m) * pair
-            spot = pl.ds(pl.multiple_of(base, pair), pair)
-
-            def keeper(start):
-                return memory_v[:, :, pl.ds(pl.multiple_of(start, pair), pair)].reshape(keys_c, pair)
-
-            part, _ = attend(crosses[:, :, spot].reshape(asked_c, pair), keeper, bias_c, base)
-            for half in range(2):
-                piece = part[half * asked_c : (half + 1) * asked_c, half * HEAD : (half + 1) * HEAD]
-                place_at = pl.ds(pl.multiple_of(base + half * HEAD, HEAD), HEAD)
-                owner_out[:, :, place_at] = piece.reshape(BEAM, quarter, HEAD)
-
-    own_back = pltpu.make_async_copy(owner_out.at[z], cross_out.at[y], local.at[2])
-    crossing = [
-        send(owner_out.at[beam], cross_out.at[y], c_send.at[beam], c_recv.at[y], dp, beam * GROUP + z)
-        for beam in range(BEAM)
-    ]
-    for beam in range(BEAM):
-        pl.when(beam * GROUP + z != ex)(crossing[beam].start)
-    pl.when(z == y)(own_back.start)
 
     paged = []
 
@@ -404,6 +405,10 @@
                 move.start()
                 sent.append(move)
 
+    if MID:
+        for off in (1, 3):
+            turn(off, EARLY, EARLY + MID, 2)
+
     def chunk(which, owner, j):
         zz = lax.rem(z + BEAM - ORDER[j], BEAM)
         return held.at[chip[which], owner, pl.ds(zz * GROUP, GROUP)]
@@ -435,7 +440,7 @@
 
     cells = picked.shape[0] // 2
     tile = min(1024, hidden)
-    wide = min(1024, width)
+    wide = min(2048, width)
     slim = min(256, width)
     band = block // 4
 
@@ -515,7 +520,7 @@
             sent.append(move)
 
     for off in (1, 3, 2):
-        begin = EARLY if off != 2 else 0
+        begin = EARLY + MID if off != 2 else 0
         turn(off, begin, PAGE_CAP, 1)
     for load in loads[6:8]:
         load.wait()
@@ -536,9 +541,9 @@
         part = chunk(OPPOSITE, core, j)
         send(part, part, o_send.at[j], o_recv.at[j], dp, ex).wait_recv()
         to_sibling(OPPOSITE, j)
+    forward(RIGHT)
     from_sibling(OPPOSITE)
     up(OPPOSITE)
-    forward(RIGHT)
     down(OPPOSITE)
     forward(OPPOSITE)
     for q in (0, 2, 1, 3):
@@ -616,7 +621,7 @@
         DMA((3,)), DMA((3,)), DMA((3,)), DMA((3,)), DMA((4,)), DMA((4,)),
         DMA((16,)), DMA((16,)), DMA((16,)), DMA((16,)),
         DMA((2, 4)), DMA((2, 4)), DMA((4,)), DMA((4,)), DMA((4, 4)), DMA((4, 4)),
-        DMA((4,)), DMA((4,)), DMA((2, 4)), DMA((2, 4)), DMA((4,)), DMA((4,)), DMA((3, 2)), DMA((3, 2)),
+        DMA((4,)), DMA((4,)), DMA((2, 4)), DMA((2, 4)), DMA((4,)), DMA((4,)), DMA((3, 3)), DMA((3, 3)),
     ]
     return pl.pallas_call(
         layer_kernel,

time: 95.4 us -> 90.8 us (0.952); the launches traced: 93.6 us -> 90.6 us
  Pallas kernels: 92.3 us -> 89.3 us
    pallas_call x1, Pallas kernels: 88.5 us -> 85.5 us  [layer(): pl.pallas_call(layer_kernel, out_shape=[jax.ShapeDtypeStruct((row_count,...]
where the time goes in v5:
time: 90.8 us; the launch traced here: 90.6 us
  Pallas kernels  89.3 us (98%)
    pallas_call x1, Pallas kernels, layer(): pl.pallas_call(layer_kernel, out_shape=[jax.ShapeDtypeStruct((row_count,...  85.5 us
    pallas_call x1, Pallas kernels, unpack(): pl.pallas_call(unpack_kernel, out_shape=jax.ShapeDtypeStruct(cache.shape,...  3.77 us

profile of v5, /device:TPU:0, one launch (start us, length us, event | category | flops | bytes accessed | tf_op | source)
XLA Modules:
  0.0 90.6 jit_solution(14938066715647306980)
XLA Ops:
  0.6 85.5 %layer.1 = (bf16[32,2048]{1,0:T(8,128)(2,1)}, bf16[3,16,8,4096]{3,2,1,0:T(8,128)(2,1)}) custom-call(bf16[32,2048]{1,0:T(8,128)(2,1)} %query.1, bf16[4,8,2048]{2,1,0:T(8,128)(2,1)} %bitcast.11, s32[1,32]{1,0:T(1,128)} %bitcast.13, s32[1,128]{1,0:T(1,128)} %bitcast.16, s32[1,8]{1,0:T(1,128)} %bitcast.17, s32[2,32]{1,0:T(2,128)} %bitcast.14, f32[2,32]{1,0:T(2,128)} %bitcast.15, ...), custom_call_target="tpu_custom_call" | custom-call | tf_op jit(solution)/shard_map/layer/pallas_call | solution.py:626
  86.2 0.0 copy-start
  86.2 3.8 %unpack.1 = bf16[32,8,4096]{2,1,0:T(8,128)(2,1)} custom-call(s32[32]{0:T(128)} %parents.1, bf16[32,8,4096]{2,1,0:T(8,128)(2,1)} %cache.3, bf16[3,16,8,4096]{3,2,1,0:T(8,128)(2,1)} %get-tuple-element.5.arrived), custom_call_target="tpu_custom_call" | custom-call | tf_op jit(solution)/shard_map/unpack/pallas_call | solution.py:71
  89.9 0.0 copy-done
  90.0 0.7 copy.17
Async XLA Ops:
  86.2 3.8 %copy-start = (bf16[32,2048]{1,0:T(8,128)(2,1)S(1)}, bf16[32,2048]{1,0:T(8,128)(2,1)}, u32[]{:S(2)}) copy-start(bf16[32,2048]{1,0:T(8,128)(2,1)} %get-tuple-element.8) | copy-start | bytes 393220

commit v6 on v5

--- a/solution.py
+++ b/solution.py
@@ -40,16 +40,20 @@
     pl.semaphore_signal(barrier, inc=1, device_id=(dp, ex), device_id_type=MESH)
 
 
-def unpack_kernel(parents, cache, arrived, fresh, sem):
+def unpack_kernel(parents, cache, arrived, rows_in, fresh, rows_out, buffer, rows_v, got, put, row_sem):
     _, _, z, _ = place()
     rows = cache.shape[0]
+    part = rows // got.shape[0]
+    take_in = pltpu.make_async_copy(rows_in, rows_v, row_sem.at[0])
+    take_in.start()
 
     def begin(row, counts):
         parent = parents[row]
         off = lax.rem(z - parent + BEAM, BEAM)
+        sem = got.at[lax.div(row, part)]
 
         def keep():
-            pltpu.make_async_copy(cache.at[row], fresh.at[row], sem).start()
+            pltpu.make_async_copy(cache.at[row], buffer.at[row], sem).start()
 
         pl.when(off == 0)(keep)
         after = []
@@ -57,32 +61,46 @@
             hit = off == step
 
             def take(step=step):
-                pltpu.make_async_copy(arrived.at[step - 1, counts[step - 1]], fresh.at[row], sem).start()
+                pltpu.make_async_copy(arrived.at[step - 1, counts[step - 1]], buffer.at[row], sem).start()
 
             pl.when(hit)(take)
             after.append(counts[step - 1] + hit.astype(jnp.int32))
         return tuple(after)
 
     lax.fori_loop(0, rows, begin, (jnp.int32(0),) * (BEAM - 1))
-    pltpu.make_async_copy(cache, fresh, sem).wait()
-
-
-def unpack(parents, cache, arrived):
+    take_in.wait()
+    give = pltpu.make_async_copy(rows_v, rows_out, row_sem.at[1])
+    give.start()
+    puts = []
+    for n in range(got.shape[0]):
+        piece = pl.ds(n * part, part)
+        pltpu.make_async_copy(cache.at[piece], buffer.at[piece], got.at[n]).wait()
+        puts.append(pltpu.make_async_copy(buffer.at[piece], fresh.at[piece], put.at[n]))
+        puts[-1].start()
+    for move in puts:
+        move.wait()
+    give.wait()
+
+
+def unpack(parents, cache, arrived, rows):
     return pl.pallas_call(
         unpack_kernel,
-        out_shape=jax.ShapeDtypeStruct(cache.shape, cache.dtype),
-        in_specs=[pl.BlockSpec(memory_space=pltpu.SMEM), ANY, ANY],
-        out_specs=pl.BlockSpec(memory_space=pltpu.VMEM),
-        scratch_shapes=[DMA],
+        out_shape=[jax.ShapeDtypeStruct(cache.shape, cache.dtype), jax.ShapeDtypeStruct(rows.shape, rows.dtype)],
+        in_specs=[pl.BlockSpec(memory_space=pltpu.SMEM), ANY, ANY, ANY],
+        out_specs=[ANY, ANY],
+        scratch_shapes=[
+            pltpu.VMEM(cache.shape, cache.dtype), pltpu.VMEM(rows.shape, rows.dtype),
+            DMA((4,)), DMA((4,)), DMA((2,)),
+        ],
         compiler_params=pltpu.CompilerParams(vmem_limit_bytes=58 * 2**20),
         name="unpack",
-    )(parents, cache, arrived)
+    )(parents, cache, arrived, rows)
 
 
 ORDER = (0, 1, 3, 2)
 OWN, LEFT, RIGHT, OPPOSITE = range(4)
 EARLY = 4
-MID = 2
+MID = 4
 
 
 def eye(n):
@@ -441,7 +459,7 @@
     cells = picked.shape[0] // 2
     tile = min(1024, hidden)
     wide = min(2048, width)
-    slim = min(256, width)
+    slim = min(1024, width)
     band = block // 4
 
     def up(which):
@@ -477,9 +495,8 @@
             to_chip[which - 1, :, spot] = both.astype(to_chip.dtype)
 
         if which == OPPOSITE:
-            for q in (0, 2, 1, 3):
-                rows = pl.ds(q * band, band)
-                relay(to_chip.at[2, rows], far.at[rows], f_send.at[q], f_recv.at[q], RIGHT if q < 2 else LEFT)
+            far_leg(0)
+            far_leg(2)
         else:
             for q in (2, 3) if which == RIGHT else (0, 1):
                 last_leg(which, q)
@@ -488,6 +505,10 @@
         move = send(src, dst, send_sem, recv_sem, chip[side] * 2 + core, ex)
         move.start()
         sent.append(move)
+
+    def far_leg(q):
+        rows = pl.ds(q * band, band)
+        relay(to_chip.at[2, rows], far.at[rows], f_send.at[q], f_recv.at[q], RIGHT if q < 2 else LEFT)
 
     def last_leg(which, q):
         rows = pl.ds(q * band, band)
@@ -499,6 +520,8 @@
         which = RIGHT if q < 2 else LEFT
         there = far.at[rows]
         send(there, there, f_send.at[q], f_recv.at[q], dp, ex).wait_recv()
+        if q in (0, 2):
+            far_leg(q + 1)
 
         @pl.loop(0, width // slim)
         def _(n):
@@ -669,7 +692,8 @@
         expert_in[0],
         expert_out[0],
     )
-    return (mixed, unpack(parents, kv_cache, arrived))
+    fresh, mixed = unpack(parents, kv_cache, arrived, mixed)
+    return (mixed, fresh)
 
 
 def solution(mesh):

time: 90.8 us -> 88.7 us (0.977); the launches traced: 90.6 us -> 87.5 us
  Pallas kernels: 89.3 us -> 86.8 us
    pallas_call x1, Pallas kernels: 85.5 us -> 83.6 us  [layer(): pl.pallas_call(layer_kernel, out_shape=[jax.ShapeDtypeStruct((row_count,...]
where the time goes in v6:
time: 88.7 us; the launch traced here: 87.5 us
  Pallas kernels  86.8 us (98%)
    pallas_call x1, Pallas kernels, layer(): pl.pallas_call(layer_kernel, out_shape=[jax.ShapeDtypeStruct((row_count,...  83.6 us
    pallas_call x1, Pallas kernels, unpack(): pl.pallas_call(unpack_kernel, out_shape=[jax.ShapeDtypeStruct(cache.shape...  3.25 us

profile of v6, /device:TPU:0, one launch (start us, length us, event | category | flops | bytes accessed | tf_op | source)
XLA Modules:
  0.0 87.5 jit_solution(9087822021632192945)
XLA Ops:
  0.6 83.6 %layer.1 = (bf16[32,2048]{1,0:T(8,128)(2,1)}, bf16[3,16,8,4096]{3,2,1,0:T(8,128)(2,1)}) custom-call(bf16[32,2048]{1,0:T(8,128)(2,1)} %query.1, bf16[4,8,2048]{2,1,0:T(8,128)(2,1)} %bitcast.11, s32[1,32]{1,0:T(1,128)} %bitcast.13, s32[1,128]{1,0:T(1,128)} %bitcast.16, s32[1,8]{1,0:T(1,128)} %bitcast.17, s32[2,32]{1,0:T(2,128)} %bitcast.14, f32[2,32]{1,0:T(2,128)} %bitcast.15, ...), custom_call_target="tpu_custom_call" | custom-call | tf_op jit(solution)/shard_map/layer/pallas_call | solution.py:649
  84.2 3.2 %unpack.1 = (bf16[32,8,4096]{2,1,0:T(8,128)(2,1)}, bf16[32,2048]{1,0:T(8,128)(2,1)}) custom-call(s32[32]{0:T(128)} %parents.1, bf16[32,8,4096]{2,1,0:T(8,128)(2,1)} %cache.3, bf16[3,16,8,4096]{3,2,1,0:T(8,128)(2,1)} %get-tuple-element.6.arrived, bf16[32,2048]{1,0:T(8,128)(2,1)} %get-tuple-element.7.rows_in), custom_call_target="tpu_custom_call" | custom-call | tf_op jit(solution)/shard_map/unpack/pallas_call | solution.py:86

commit v7 on v6

--- a/solution.py
+++ b/solution.py
@@ -458,7 +458,7 @@
 
     cells = picked.shape[0] // 2
     tile = min(1024, hidden)
-    wide = min(2048, width)
+    wide = min(1024, width)
     slim = min(1024, width)
     band = block // 4
 
@@ -473,24 +473,25 @@
             inner[:, spot] = jnp.maximum(part, 0.0).astype(inner.dtype)
 
     def down(which):
-        @pl.loop(0, width // wide)
-        def _(n):
-            spot = pl.ds(pl.multiple_of(n * wide, wide), wide)
+        for n in range(width // wide):
+            spot = slice(n * wide, (n + 1) * wide)
             part = jnp.dot(inner[...], second_v[:, spot], preferred_element_type=jnp.float32)
             total[which, :, spot] = part[:cells]
             to_twin[which, :, spot] = part[cells:].astype(to_twin.dtype)
-
-        move = send(to_twin.at[which], from_twin.at[which], y_send.at[which], y_recv.at[which], twin, ex)
-        move.start()
-        sent.append(move)
+            move = twin_half(which, n)
+            move.start()
+            sent.append(move)
+
+    def twin_half(which, n):
+        spot = pl.ds(n * wide, wide)
+        return send(
+            to_twin.at[which, :, spot], from_twin.at[which, :, spot], y_send.at[which, n], y_recv.at[which, n], twin, ex
+        )
 
     def forward(which):
-        there = from_twin.at[which]
-        send(there, there, y_send.at[which], y_recv.at[which], twin, ex).wait_recv()
-
-        @pl.loop(0, width // slim)
-        def _(n):
-            spot = pl.ds(pl.multiple_of(n * slim, slim), slim)
+        for n in range(width // wide):
+            twin_half(which, n).wait_recv()
+            spot = slice(n * wide, (n + 1) * wide)
             both = total[which, :, spot] + from_twin[which, :, spot].astype(jnp.float32)
             to_chip[which - 1, :, spot] = both.astype(to_chip.dtype)
 
@@ -572,8 +573,8 @@
     for q in (0, 2, 1, 3):
         merge(q)
 
-    there = from_twin.at[OWN]
-    send(there, there, y_send.at[OWN], y_recv.at[OWN], twin, ex).wait_recv()
+    for n in range(width // wide):
+        twin_half(OWN, n).wait_recv()
     stay = pltpu.make_async_copy(result.at[ex], returned.at[ex], local.at[1])
     for q in (0, 2, 1, 3):
         rows = pl.ds(q * band, band)
@@ -644,7 +645,7 @@
         DMA((3,)), DMA((3,)), DMA((3,)), DMA((3,)), DMA((4,)), DMA((4,)),
         DMA((16,)), DMA((16,)), DMA((16,)), DMA((16,)),
         DMA((2, 4)), DMA((2, 4)), DMA((4,)), DMA((4,)), DMA((4, 4)), DMA((4, 4)),
-        DMA((4,)), DMA((4,)), DMA((2, 4)), DMA((2, 4)), DMA((4,)), DMA((4,)), DMA((3, 3)), DMA((3, 3)),
+        DMA((4, 2)), DMA((4, 2)), DMA((2, 4)), DMA((2, 4)), DMA((4,)), DMA((4,)), DMA((3, 3)), DMA((3, 3)),
     ]
     return pl.pallas_call(
         layer_kernel,

time: 88.7 us -> 88.8 us (level)
  no operation moved by 1% of the time
where the time goes in v7:
time: 88.8 us; the launch traced here: 87.4 us
  Pallas kernels  86.8 us (98%)
    pallas_call x1, Pallas kernels, layer(): pl.pallas_call(layer_kernel, out_shape=[jax.ShapeDtypeStruct((row_count,...  83.6 us
    pallas_call x1, Pallas kernels, unpack(): pl.pallas_call(unpack_kernel, out_shape=[jax.ShapeDtypeStruct(cache.shape...  3.25 us

profile of v7, /device:TPU:0, one launch (start us, length us, event | category | flops | bytes accessed | tf_op | source)
XLA Modules:
  0.0 87.4 jit_solution(16704364086230296501)
XLA Ops:
  0.6 83.6 %layer.1 = (bf16[32,2048]{1,0:T(8,128)(2,1)}, bf16[3,16,8,4096]{3,2,1,0:T(8,128)(2,1)}) custom-call(bf16[32,2048]{1,0:T(8,128)(2,1)} %query.1, bf16[4,8,2048]{2,1,0:T(8,128)(2,1)} %bitcast.11, s32[1,32]{1,0:T(1,128)} %bitcast.13, s32[1,128]{1,0:T(1,128)} %bitcast.16, s32[1,8]{1,0:T(1,128)} %bitcast.17, s32[2,32]{1,0:T(2,128)} %bitcast.14, f32[2,32]{1,0:T(2,128)} %bitcast.15, ...), custom_call_target="tpu_custom_call" | custom-call | tf_op jit(solution)/shard_map/layer/pallas_call | solution.py:650
  84.2 3.2 %unpack.1 = (bf16[32,8,4096]{2,1,0:T(8,128)(2,1)}, bf16[32,2048]{1,0:T(8,128)(2,1)}) custom-call(s32[32]{0:T(128)} %parents.1, bf16[32,8,4096]{2,1,0:T(8,128)(2,1)} %cache.3, bf16[3,16,8,4096]{3,2,1,0:T(8,128)(2,1)} %get-tuple-element.6.arrived, bf16[32,2048]{1,0:T(8,128)(2,1)} %get-tuple-element.7.rows_in), custom_call_target="tpu_custom_call" | custom-call | tf_op jit(solution)/shard_map/unpack/pallas_call | solution.py:86
